TPU v7x, 32 devices: a whole 2x2x4 slice. The times are simulated.
32 devices in a mesh: group: 4 (over y, core), dev: 8 (over z, x).
Axes of the slice: x: 2, y: 2, z: 4, core: 2. Of those that a mesh axis runs over, the one named last changes fastest.
Arguments:
- features_in: bfloat16 [96, 32768], P(None, ('group', 'dev')), may hold values from -6 to 6
- occupancy: int32 [32768], P(('group', 'dev')), may hold values 0 or 1
- cotangent: bfloat16 [96, 32768], P(None, ('group', 'dev')), may hold values from -6 to 6
- kernel_one: bfloat16 [27, 96, 96], replicated, may hold values from -0.125 to 0.125
- kernel_two: bfloat16 [27, 96, 96], replicated, may hold values from -0.125 to 0.125
- neighbours: int32 [64, 27], P(('group', 'dev')), may hold values from -1 to 5, as said below
Outputs:
- features_out: bfloat16 [96, 32768], P(None, ('group', 'dev'))
- kernel_one_grad: float32 [27, 96, 96], replicated
- kernel_two_grad: float32 [27, 96, 96], replicated
Inputs may be any that keep to these rules, and one draw needn't show every extreme that they name: `neighbours`: the blocks of a device sit at distinct places of a 4 by 4 grid in y and z; the device's dev index is its slab's x position in the region. Entry 13 of a block is its own index. Other entries are -1 where no block lies at that offset (always beyond the first and last device of a region), n < 2 for block n of the same device, 2 + n for block n of the device with dev index one lower, 4 + n for block n of the device with dev index one higher; only offsets with dx = -1 or 1 reach other devices. The relation is mutual: entry t of block a names block b exactly when entry 26 - t of b names a.
All inputs are finite; a program needn't handle non-finite values. No bound on the sum of `occupancy` on one device may be relied on, other than what follows from the above.
Results may differ from a plain program's by a relative error of at most 0.0049.
Values may be sent and summed in bfloat16 or wider, within the bound.
A program may use at most 64 MiB of HBM per device.

v0:
```python
import jax
import jax.numpy as jnp
import numpy as np
from jax import lax
from jax.sharding import PartitionSpec as P


def with_halo(block, sides, width):
    for axis, dim in sides:
        count = lax.axis_size(axis)
        forward = [(i, i + 1) for i in range(count - 1)]
        backward = [(target, source) for source, target in forward]
        low = lax.ppermute(
            lax.slice_in_dim(block, block.shape[dim] - width, None, axis=dim), axis, forward
        )
        high = lax.ppermute(lax.slice_in_dim(block, 0, width, axis=dim), axis, backward)
        block = jnp.concatenate([low, block, high], axis=dim)
    return block


def pad_tables():
    cells = np.arange(1000)
    coord_x = cells // 100
    coord_y = cells // 10 % 10
    coord_z = cells % 10

    def side(coord):
        return np.where(coord == 0, -1, np.where(coord == 9, 1, 0))

    def inner(coord):
        return np.where(coord == 0, 7, np.where(coord == 9, 0, coord - 1))

    offset_of = (side(coord_x) + 1) * 9 + (side(coord_y) + 1) * 3 + (side(coord_z) + 1)
    voxel_of = inner(coord_x) * 64 + inner(coord_y) * 8 + inner(coord_z)
    return (offset_of.astype(np.int32), voxel_of.astype(np.int32))


def cube_window(cube, first, second, third, width):
    return cube[:, :, first : first + 8, second : second + 8, third : third + 8].reshape(width, -1)


def conv_forward(padded, kernel):
    width = padded.shape[0]
    cube = padded.reshape(width, -1, 10, 10, 10)
    total = None
    for first in range(3):
        for second in range(3):
            stacked = jnp.concatenate(
                [cube_window(cube, first, second, third, width) for third in range(3)], axis=0
            )
            start = first * 9 + second * 3
            weights = kernel[start : start + 3].reshape(3 * width, width)
            term = lax.dot_general(
                weights, stacked, (((0,), (0,)), ((), ())), preferred_element_type=jnp.float32
            )
            total = term if total is None else total + term
    return total


def kernel_terms(padded, grad):
    width = padded.shape[0]
    cube = padded.reshape(width, -1, 10, 10, 10)
    pieces = []
    for first in range(3):
        for second in range(3):
            stacked = jnp.concatenate(
                [cube_window(cube, first, second, third, width) for third in range(3)], axis=0
            )
            term = lax.dot_general(
                stacked, grad, (((1,), (1,)), ((), ())), preferred_element_type=jnp.float32
            )
            pieces.append(term.reshape(3, width, width))
    return jnp.concatenate(pieces, axis=0)


def conv_backward(padded, kernel):
    width = padded.shape[0]
    cube = padded.reshape(width, -1, 10, 10, 10)
    total = None
    for first in range(3):
        for second in range(3):
            stacked = jnp.concatenate(
                [cube_window(cube, 2 - first, 2 - second, 2 - third, width) for third in range(3)],
                axis=0,
            )
            start = first * 9 + second * 3
            weights = jnp.concatenate([kernel[start + third] for third in range(3)], axis=1)
            term = jnp.dot(weights, stacked, preferred_element_type=jnp.float32)
            total = term if total is None else total + term
    return total


def rims_beside(values, which):
    if which == "inputs":
        arrived = with_halo(values[None], (("dev", 0),), 1)
    else:
        arrived = with_halo(values[None], (("dev", 0),), 1)
    return (arrived[0], arrived[2], 512)


def padded_of(values, lower, upper, stride, neighbours):
    offset_np, voxel_np = pad_tables()
    offset_of = jnp.asarray(offset_np)
    voxel_of = jnp.asarray(voxel_np)
    inner_of = voxel_of % stride
    blocks_here = neighbours.shape[0]
    local_span = blocks_here * 512
    rim_span = blocks_here * stride
    entries = neighbours[:, offset_of]
    local_col = entries * 512 + voxel_of[None, :]
    lower_col = local_span + (entries - blocks_here) * stride + inner_of[None, :]
    upper_col = local_span + rim_span + (entries - 2 * blocks_here) * stride + inner_of[None, :]
    zero_col = local_span + 2 * rim_span
    columns = jnp.where(
        entries < blocks_here, local_col, jnp.where(entries < 2 * blocks_here, lower_col, upper_col)
    )
    columns = jnp.where(entries < 0, zero_col, columns)
    table = jnp.concatenate(
        [values, lower, upper, jnp.zeros((values.shape[0], 1), values.dtype)], axis=1
    )
    return jnp.take(table, columns.reshape(-1), axis=1)


def reduce_grad(grad):
    flat = grad.reshape(-1)
    whole = lax.psum(flat, ("group", "dev"))
    return whole.reshape(grad.shape)


def per_device(features_in, occupancy, cotangent, kernel_one, kernel_two, neighbours):
    width = features_in.shape[0]
    mask = occupancy.astype(jnp.float32)[None, :]
    occupied = occupancy[None, :] > 0
    total_voxels = features_in.shape[1] * lax.axis_size("group") * lax.axis_size("dev")
    scale = float(total_voxels) ** (-0.5)
    a_zero = jnp.where(occupied, features_in, jnp.zeros_like(features_in))
    g_two = jnp.where(occupied, cotangent, jnp.zeros_like(cotangent))
    both = jnp.concatenate([a_zero, g_two], axis=0)
    lower, upper, stride = rims_beside(both, "inputs")
    padded_both = padded_of(both, lower, upper, stride, neighbours)
    padded_zero = padded_both[:width]
    padded_grad = padded_both[width:]
    z_one = mask * conv_forward(padded_zero, kernel_one)
    a_one = jax.nn.silu(z_one).astype(jnp.bfloat16)
    lower, upper, stride = rims_beside(a_one, "hidden")
    padded_one = padded_of(a_one, lower, upper, stride, neighbours)
    features_out = (mask * conv_forward(padded_one, kernel_two)).astype(jnp.bfloat16)
    kernel_two_grad = reduce_grad(scale * kernel_terms(padded_one, g_two))
    ga_one = mask * conv_backward(padded_grad, kernel_two)
    sigma = jax.nn.sigmoid(z_one)
    gz_one = (ga_one * sigma * (1.0 + z_one * (1.0 - sigma))).astype(jnp.bfloat16)
    kernel_one_grad = reduce_grad(scale * kernel_terms(padded_zero, gz_one))
    return (features_out, kernel_one_grad, kernel_two_grad)


def solution(mesh):
    return jax.shard_map(
        per_device,
        mesh=mesh,
        in_specs=(
            P(None, ("group", "dev")),
            P(("group", "dev")),
            P(None, ("group", "dev")),
            P(),
            P(),
            P(("group", "dev"), None),
        ),
        out_specs=(P(None, ("group", "dev")), P(), P()),
        check_vma=False,
    )
```

profile of v0, /device:TPU:0, one launch (start us, length us, event | category | flops | bytes accessed | tf_op | source)
XLA Modules:
  0.0 263.7 jit_solution(3492124967742507906)
XLA Ops:
  7.2 0.7 broadcast_compare_fusion
  8.0 1.1 copy.37
  9.1 1.1 copy.38
  10.7 1.3 collective-permute-start.1
  12.0 6.3 %collective-permute-start = (bf16[1,192,1024]{1,2,0:T(8,128)(2,1)S(1)}, bf16[1,192,1024]{1,2,0:T(8,128)(2,1)}, u32[]{:S(2)}, u32[]{:S(2)}) collective-permute-start(bf16[1,192,1024]{1,2,0:T(8,128)(2,1)S(1)} %maximum_bitcast_fusion), channel_id=1, source_target_pairs={{0,1},{1,2},{2,3},{3,4},{4,5},{5,6},{6,7},{8,9},{9,10},{10,11},{11... | collective-permute-start | bytes 1179656 | tf_op jit(solution)/shard_map/ppermute | solution.py:13
  18.2 0.7 slice_bitcast_fusion.1
  18.9 0.8 slice_bitcast_fusion.2
  19.9 2.9 %gather_fusion = s32[1000,2]{1,0:T(8,128)S(1)} fusion(s32[2,27]{0,1:T(8,128)S(1)} %copy.30, s32[1024]{0:T(1024)S(1)} %pad_clamp_fusion.1), kind=kCustom, calls=%fused_computation | custom fusion | bytes 20000 | tf_op jit(solution)/shard_map/gather | solution.py:109
  23.3 0.8 fusion.172
  24.1 0.8 fusion.173
  26.6 1.0 collective-permute-done.1
  27.5 11.3 %collective-permute-done = bf16[1,192,1024]{1,2,0:T(8,128)(2,1)} collective-permute-done((bf16[1,192,1024]{1,2,0:T(8,128)(2,1)S(1)}, bf16[1,192,1024]{1,2,0:T(8,128)(2,1)}, u32[]{:S(2)}, u32[]{:S(2)}) %collective-permute-start) | collective-permute-done | bytes 393248 | tf_op jit(solution)/shard_map/ppermute | solution.py:13
  38.8 4.9 %maximum_maximum_fusion = bf16[192,3073]{0,1:T(8,128)(2,1)S(1)} fusion(bf16[192,1024]{0,1:T(8,128)(2,1)} %bitcast.8, bf16[192,1024]{0,1:T(8,128)(2,1)} %bitcast.7, bf16[96,1024]{0,1:T(8,128)(2,1)S(1)} %get-tuple-element.141, bf16[96,1024]{0,1:T(8,128)(2,1)S(1)} %get-tuple-element.140, bf16[3073]{0:T(1024)(128)(2,1)S(1)} %pad.116.clone), kind=kLoop, calls=%fused_computation.3 | loop fusion | flops 5900160 | bytes 2365826 | tf_op jit(solution)/shard_map/concatenate | solution.py:118
  43.7 7.9 %gather_fusion.1 = bf16[2000,192]{1,0:T(8,128)(2,1)S(1)} fusion(bf16[192,3073]{0,1:T(8,128)(2,1)S(1)} %maximum_maximum_fusion, s32[2048]{0:T(1024)S(1)} %pad_clamp_fusion), kind=kCustom, calls=%fused_computation.1 | custom fusion | bytes 1544000 | tf_op jit(solution)/shard_map/jit(_take)/gather | solution.py:121
  52.4 1.3 fusion.167
  53.6 2.4 fusion.166
  56.7 1.0 fusion.170
  57.7 0.6 fusion.74
  58.6 0.6 convolution_add_fusion.23
  59.3 0.6 convolution_add_fusion.22
  60.1 0.6 convolution_add_fusion.21
  60.8 0.6 convolution_add_fusion.20
  61.7 0.6 convolution_add_fusion.19
  62.3 0.6 convolution_add_fusion.18
  63.0 0.6 convolution_add_fusion.17
  64.3 0.7 multiply_convert_fusion
  69.7 0.8 convolution_add_fusion.2
  72.1 0.8 fusion.63
  72.9 0.8 fusion.64
  73.6 0.8 fusion.65
  74.4 0.8 fusion.66
  75.2 0.8 fusion.67
  76.0 0.8 fusion.68
  76.8 0.8 fusion.69
  77.5 0.8 fusion.70
  78.3 0.8 fusion.73
  79.1 1.3 collective-permute-start.3
  80.4 5.1 %collective-permute-start.2 = (bf16[1,96,1024]{2,1,0:T(8,128)(2,1)S(1)}, bf16[1,96,1024]{2,1,0:T(8,128)(2,1)S(1)}, u32[]{:S(2)}, u32[]{:S(2)}) collective-permute-start(bf16[1,96,1024]{2,1,0:T(8,128)(2,1)S(1)} %bitcast.388), channel_id=1, source_target_pairs={{0,1},{1,2},{2,3},{3,4},{4,5},{5,6},{6,7},{8,9},{9,10},{10,11},{11... | collective-permute-start | bytes 589832 | tf_op jit(solution)/shard_map/ppermute | solution.py:13
  85.7 2.9 %collective-permute-done.3 = bf16[1,96,1024]{2,1,0:T(8,128)(2,1)S(1)} collective-permute-done((bf16[1,96,1024]{2,1,0:T(8,128)(2,1)S(1)}, bf16[1,96,1024]{2,1,0:T(8,128)(2,1)S(1)}, u32[]{:S(2)}, u32[]{:S(2)}) %collective-permute-start.3) | collective-permute-done | bytes 196640 | tf_op jit(solution)/shard_map/ppermute | solution.py:16
  88.7 4.4 %collective-permute-done.2 = bf16[1,96,1024]{2,1,0:T(8,128)(2,1)S(1)} collective-permute-done((bf16[1,96,1024]{2,1,0:T(8,128)(2,1)S(1)}, bf16[1,96,1024]{2,1,0:T(8,128)(2,1)S(1)}, u32[]{:S(2)}, u32[]{:S(2)}) %collective-permute-start.2) | collective-permute-done | bytes 196640 | tf_op jit(solution)/shard_map/ppermute | solution.py:13
  93.6 6.3 %gather_fusion.2 = bf16[2000,96]{1,0:T(8,128)(2,1)S(1)} fusion(bf16[96,3073]{0,1:T(8,128)(2,1)S(1)} %copy.39, s32[2048]{0:T(1024)S(1)} %pad_clamp_fusion), kind=kCustom, calls=%fused_computation.2 | custom fusion | bytes 776000 | tf_op jit(solution)/shard_map/jit(_take)/gather | solution.py:121
  100.2 0.9 broadcast_select_fusion
  101.5 0.8 fusion.168
  102.3 0.8 fusion.71
  103.9 0.8 fusion.62
  104.8 0.6 convolution_add_fusion.15
  105.5 0.8 fusion.61
  106.3 0.6 convolution_add_fusion.14
  107.0 0.8 fusion.60
  107.8 1.4 convolution_add_fusion.13
  109.2 0.8 fusion.59
  110.0 0.8 fusion.58
  110.8 0.8 fusion.57
  111.6 0.8 fusion.56
  112.4 0.8 fusion.55
  113.7 1.7 broadcast_multiply_fusion
  115.5 0.9 copy-done.30
  116.4 1.7 convolution_add_fusion.12
  118.2 0.6 convolution_add_fusion.11
  119.7 0.6 convolution_add_fusion.9
  120.4 1.3 fusion.8
  121.6 131.1 %all-reduce.3.cloned.1.call-done = (f32[27,96,96]{2,1,0:T(8,128)}, f32[27,96,96]{2,1,0:T(8,128)}) async-done(((f32[27,96,96]{2,1,0:T(8,128)}, f32[27,96,96]{2,1,0:T(8,128)}), (f32[27,96,96]{2,1,0:T(8,128)}, f32[27,96,96]{2,1,0:T(8,128)})) %all-reduce.3.cloned.1.call-update) | async-done | bytes 1990672 | tf_op jit(solution)/shard_map/psum | solution.py:126
  252.8 2.6 copy.58
  255.4 1.1 copy.59
  (215 shorter events, 15.4 us)
Async XLA Ops:
  7.2 11.1 %copy-start = (bf16[27,96,96]{2,1,0:T(8,128)(2,1)S(1)}, bf16[27,96,96]{2,1,0:T(8,128)(2,1)}, u32[]{:S(2)}) copy-start(bf16[27,96,96]{2,1,0:T(8,128)(2,1)} %param.14) | copy-start | bytes 1492996
  7.2 245.6 %all-reduce.3.cloned.1.call-start = ((), (), s32[]{:S(2)}) async-start(), calls=%async_computation | async-start | bytes 5308416 | tf_op jit(solution)/shard_map/psum | solution.py:126
  10.2 9.6 %copy-start.75 = (s32[1000]{0:T(1024)S(1)}, s32[1000]{0:T(1024)}, u32[]{:S(2)}) copy-start(s32[1000]{0:T(1024)} %constant.102) | copy-start | bytes 12004
  10.2 9.6 %copy-start.77 = (s32[2,27]{1,0:T(2,128)S(1)}, s32[2,27]{1,0:T(2,128)}, u32[]{:S(2)}) copy-start(s32[2,27]{1,0:T(2,128)} %param.15) | copy-start | bytes 652
  10.4 12.6 %copy-start.76 = (s32[1000]{0:T(1024)S(1)}, s32[1000]{0:T(1024)}, u32[]{:S(2)}) copy-start(s32[1000]{0:T(1024)} %constant.83.clone) | copy-start | bytes 12004
  10.7 16.9 %collective-permute-start.1 = (bf16[1,192,1024]{1,2,0:T(8,128)(2,1)S(1)}, bf16[1,192,1024]{1,2,0:T(8,128)(2,1)}, u32[]{:S(2)}, u32[]{:S(2)}) collective-permute-start(bf16[1,192,1024]{1,2,0:T(8,128)(2,1)S(1)} %maximum_bitcast_fusion), channel_id=1, source_target_pairs={{1,0},{2,1},{3,2},{4,3},{5,4},{6,5},{7,6},{9,8},{10,9},{11,10},{12... | collective-permute-start | bytes 1179656 | tf_op jit(solution)/shard_map/ppermute | solution.py:16
  12.0 26.8 %collective-permute-start = (bf16[1,192,1024]{1,2,0:T(8,128)(2,1)S(1)}, bf16[1,192,1024]{1,2,0:T(8,128)(2,1)}, u32[]{:S(2)}, u32[]{:S(2)}) collective-permute-start(bf16[1,192,1024]{1,2,0:T(8,128)(2,1)S(1)} %maximum_bitcast_fusion), channel_id=1, source_target_pairs={{0,1},{1,2},{2,3},{3,4},{4,5},{5,6},{6,7},{8,9},{9,10},{10,11},{11... | collective-permute-start | bytes 1179656 | tf_op jit(solution)/shard_map/ppermute | solution.py:13
  18.9 5.1 %copy-start.4 = (bf16[27,96,96]{2,1,0:T(8,128)(2,1)S(1)}, bf16[27,96,96]{2,1,0:T(8,128)(2,1)}, u32[]{:S(2)}) copy-start(bf16[27,96,96]{2,1,0:T(8,128)(2,1)} %param.13) | copy-start | bytes 1492996
  22.8 2.0 copy-start.72
  23.2 3.2 %copy-start.32 = (s32[10,10,10]{2,1,0:T(8,128)S(1)}, s32[10,10,10]{2,1,0:T(8,128)}, u32[]{:S(2)}) copy-start(s32[10,10,10]{2,1,0:T(8,128)} %constant.89) | copy-start | bytes 12004
  56.7 1.1 copy-start.44
  64.3 1.0 copy-start.25
  64.3 1.1 copy-start.26
  64.3 1.1 copy-start.47
  64.3 1.1 copy-start.48
  64.3 1.1 copy-start.49
  65.0 1.0 copy-start.21
  65.0 1.1 copy-start.22
  65.0 1.1 copy-start.23
  65.0 1.1 copy-start.69
  65.0 1.1 copy-start.70
  65.0 1.1 copy-start.71
  66.0 1.0 copy-start.18
  66.0 1.1 copy-start.19
  66.0 1.1 copy-start.20
  66.0 1.1 copy-start.66
  66.0 1.1 copy-start.67
  66.0 1.1 copy-start.68
  66.7 1.0 copy-start.15
  66.8 1.1 copy-start.16
  66.8 1.2 copy-start.17
  66.8 1.1 copy-start.63
  66.8 1.1 copy-start.64
  66.8 1.1 copy-start.65
  67.7 1.0 copy-start.12
  67.7 1.1 copy-start.13
  67.7 1.1 copy-start.14
  67.7 1.1 copy-start.60
  67.7 1.1 copy-start.61
  67.8 1.1 copy-start.62
  68.5 1.0 copy-start.9
  68.5 1.1 copy-start.10
  68.5 1.2 copy-start.11
  68.5 1.1 copy-start.57
  68.5 1.1 copy-start.58
  68.5 1.1 copy-start.59
  69.5 1.1 copy-start.6
  69.5 1.1 copy-start.7
  69.5 1.1 copy-start.8
  69.5 1.1 copy-start.54
  69.5 1.1 copy-start.55
  69.5 1.1 copy-start.56
  70.5 1.0 copy-start.5
  70.5 1.0 copy-start.45
  79.1 9.6 %collective-permute-start.3 = (bf16[1,96,1024]{2,1,0:T(8,128)(2,1)S(1)}, bf16[1,96,1024]{2,1,0:T(8,128)(2,1)S(1)}, u32[]{:S(2)}, u32[]{:S(2)}) collective-permute-start(bf16[1,96,1024]{2,1,0:T(8,128)(2,1)S(1)} %bitcast.387), channel_id=1, source_target_pairs={{1,0},{2,1},{3,2},{4,3},{5,4},{6,5},{7,6},{9,8},{10,9},{11,10},{12... | collective-permute-start | bytes 589832 | tf_op jit(solution)/shard_map/ppermute | solution.py:16
  80.4 12.6 %collective-permute-start.2 = (bf16[1,96,1024]{2,1,0:T(8,128)(2,1)S(1)}, bf16[1,96,1024]{2,1,0:T(8,128)(2,1)S(1)}, u32[]{:S(2)}, u32[]{:S(2)}) collective-permute-start(bf16[1,96,1024]{2,1,0:T(8,128)(2,1)S(1)} %bitcast.388), channel_id=1, source_target_pairs={{0,1},{1,2},{2,3},{3,4},{4,5},{5,6},{6,7},{8,9},{9,10},{10,11},{11... | collective-permute-start | bytes 589832 | tf_op jit(solution)/shard_map/ppermute | solution.py:13
  85.7 7.3 %copy-start.1 = (f32[27,96,96]{2,1,0:T(8,128)}, f32[27,96,96]{2,1,0:T(8,128)S(1)}, u32[]{:S(2)}) copy-start(f32[27,96,96]{2,1,0:T(8,128)S(1)} %constant_dynamic-update-slice_fusion) | copy-start | bytes 2985988
  102.3 6.9 %copy-start.29 = (bf16[96,2,8,8,8]{0,4,3,2,1:T(8,128)(2,1)}, bf16[96,2,8,8,8]{0,4,3,2,1:T(8,128)(2,1)S(1)}, u32[]{:S(2)}) copy-start(bf16[96,2,8,8,8]{0,4,3,2,1:T(8,128)(2,1)S(1)} %get-tuple-element.51) | copy-start | bytes 589828
  102.3 6.9 %copy-start.31 = (bf16[96,2,8,8,8]{0,4,3,2,1:T(8,128)(2,1)}, bf16[96,2,8,8,8]{0,4,3,2,1:T(8,128)(2,1)S(1)}, u32[]{:S(2)}) copy-start(bf16[96,2,8,8,8]{0,4,3,2,1:T(8,128)(2,1)S(1)} %get-tuple-element.52) | copy-start | bytes 589828
  102.3 7.7 %copy-start.27 = (bf16[96,2,8,8,8]{0,4,3,2,1:T(8,128)(2,1)}, bf16[96,2,8,8,8]{0,4,3,2,1:T(8,128)(2,1)S(1)}, u32[]{:S(2)}) copy-start(bf16[96,2,8,8,8]{0,4,3,2,1:T(8,128)(2,1)S(1)} %get-tuple-element.49) | copy-start | bytes 589828
  112.4 1.3 copy-start.2
  115.5 2.7 %copy-start.28 = (bf16[96,2,8,8,8]{0,4,3,2,1:T(8,128)(2,1)S(1)}, bf16[96,2,8,8,8]{0,4,3,2,1:T(8,128)(2,1)}, u32[]{:S(2)}) copy-start(bf16[96,2,8,8,8]{0,4,3,2,1:T(8,128)(2,1)} %copy-done.27) | copy-start | bytes 589828
  115.5 2.7 %copy-start.34 = (bf16[3,96,96]{2,1,0:T(8,128)(2,1)S(1)}, bf16[3,96,96]{2,1,0:T(8,128)(2,1)}, u32[]{:S(2)}) copy-start(bf16[3,96,96]{2,1,0:T(8,128)(2,1)} %get-tuple-element.122) | copy-start | bytes 165892
  252.8 2.6 copy-start.3
  (19 other events, 16.4 us)
Sparse Core Ops, SparseCore 0:
  115.6 137.1 all-reduce.2
where the time goes:
time: 269 us; the launch traced here: 264 us
  waiting for transfers between devices  151 us (56%)
  local copies, waits for them, and re-layouts  40.2 us (15%)
  matrix products  33 us (12%)
  between operations  15.8 us (6%)
  starting transfers between devices  14 us (5%)
  other arithmetic  9.91 us (4%)
    psum x1, waiting for transfers between devices, reduce_grad(): whole = lax.psum(flat, ('group', 'dev'))  131 us
    ppermute x2, waiting for transfers between devices, with_halo(): lax.ppermute(lax.slice_in_dim(block, block.shape[dim] - width, None, axis...  15.6 us
    gather x3, local copies, waits for them, and re-layouts, padded_of(): return jnp.take(table, columns.reshape(-1), axis=1)  14.4 us
    dot_general x18, matrix products, kernel_terms(): lax.dot_general(stacked, grad, (((1,), (1,)), ((), ())), preferred_elemen...  13.9 us
    dot_general x18, matrix products, conv_forward(): lax.dot_general(weights, stacked, (((0,), (0,)), ((), ())), preferred_ele...  13.7 us
    ppermute x2, starting transfers between devices, with_halo(): lax.ppermute(lax.slice_in_dim(block, block.shape[dim] - width, None, axis...  11.4 us
    unnamed x177, local copies, waits for them, and re-layouts  11.1 us
    slice x6, local copies, waits for them, and re-layouts, cube_window(): cube[:, :, first:first + 8, second:second + 8, third:third + 8]  6.39 us
  transfers between devices with their start and end apart: 5, of which 5 were waited for; matrix products, arithmetic and copies ran while one was open for 5% of the time, Pallas kernels for 0%

commit v1 on v0

v1 whole, which is shorter than its diff:
```python
import functools
import math

import jax
import jax.numpy as jnp
from jax import lax
from jax.experimental import pallas as pl
from jax.experimental.pallas import tpu as pltpu
from jax.sharding import PartitionSpec as P

LANES = 128
TAPS = 27
PLANE = 64
F32 = jnp.float32
BF16 = jnp.bfloat16


def build_windows(blocks, local, lower, upper, near, q, cols):
    row = lax.broadcasted_iota(jnp.int32, (1, 8, LANES), 1)

    def shifted(main, before, after):
        down = jnp.where(row == 0, pltpu.roll(before, 1, 1), pltpu.roll(main, 1, 1))
        up = jnp.where(row == 7, pltpu.roll(after, 7, 1), pltpu.roll(main, 7, 1))
        return down, main, up

    for b in range(blocks):
        for tx in range(3):
            for ty in range(3):
                src_y = (slice(7, 8), slice(0, 8), slice(0, 1))[ty]
                dst_y = (slice(0, 1), slice(1, 9), slice(9, 10))[ty]
                dst_x = (slice(0, 1), slice(1, 9), slice(9, 10))[tx]
                rows_y = src_y.stop - src_y.start
                rows_x = dst_x.stop - dst_x.start
                parts = []
                for tz in range(3):
                    n = near[b, tx * 9 + ty * 3 + tz]
                    if tx == 1:
                        index = jnp.where(n < 0, blocks, n)
                        value = local[index, :, src_y]
                    elif tx == 0:
                        index = jnp.where(n < 0, blocks, n - blocks)
                        value = lower[index, src_y]
                    else:
                        index = jnp.where(n < 0, blocks, n - 2 * blocks)
                        value = upper[index, src_y]
                    parts.append(value.reshape(rows_x * rows_y, 8, LANES))
                moved = shifted(parts[1], parts[0], parts[2])
                for dz in range(3):
                    q[dz, b, dst_x, dst_y] = moved[dz].reshape(rows_x, rows_y, 8, LANES)
        for dy in range(3):
            for dz in range(3):
                k = dy * 3 + dz
                window = q[dz, b, :, dy : dy + 8].reshape(10 * PLANE, LANES)
                cols[b, :, k * LANES : (k + 1) * LANES] = window.astype(BF16)


def tall(values, width):
    values = values.astype(F32)
    filler = jnp.zeros((LANES - width, values.shape[1]), F32)
    return jnp.concatenate([values, filler], axis=0).T


def first_kernel(
    blocks, width, feat, cot, occ, low_in, high_in, one, two, near,
    a_out, rim_first, rim_last, terms,
    local, rims, q, cols_a, cols_g, weight_one, weight_two, spread,
):
    taps = 9 * LANES
    span = 8 * PLANE
    mask_row = (occ[...] > 0).astype(F32)
    mask = jnp.broadcast_to(mask_row, (LANES, blocks * span)).T
    for kind, source in ((0, feat), (1, cot)):
        value = tall(source[...].astype(F32) * mask_row, width)
        local[kind, 0:blocks] = value.reshape(blocks, 8, 8, 8, LANES)
        local[kind, blocks] = jnp.zeros((8, 8, 8, LANES), F32)
        for side, arrived in ((0, low_in), (1, high_in)):
            rim = tall(arrived[kind * width : (kind + 1) * width, :], width)
            rims[kind, side, 0:blocks] = rim.reshape(blocks, 8, 8, LANES)
            rims[kind, side, blocks] = jnp.zeros((8, 8, LANES), F32)
    weight_one[...] = jnp.zeros_like(weight_one)
    weight_two[...] = jnp.zeros_like(weight_two)
    for t in range(TAPS):
        weight_one[t * LANES : t * LANES + width, 0:width] = one[t]
        weight_two[0:width, t * LANES : t * LANES + width] = two[TAPS - 1 - t]
    spread[...] = jnp.zeros_like(spread)

    build_windows(blocks, local.at[0], rims.at[0, 0], rims.at[0, 1], near, q, cols_a)
    build_windows(blocks, local.at[1], rims.at[1, 0], rims.at[1, 1], near, q, cols_g)
    for b in range(blocks):
        z = jnp.zeros((span, LANES), F32)
        ga = jnp.zeros((span, LANES), F32)
        for dx in range(3):
            rows = slice(dx * PLANE, dx * PLANE + span)
            z += jnp.dot(
                cols_a[b, rows, :],
                weight_one[dx * taps : (dx + 1) * taps, :],
                preferred_element_type=F32,
            )
            ga += lax.dot_general(
                cols_g[b, rows, :],
                weight_two[:, dx * taps : (dx + 1) * taps],
                (((1,), (1,)), ((), ())),
                preferred_element_type=F32,
            )
        inside = mask[b * span : (b + 1) * span]
        z = z * inside
        ga = ga * inside
        sigma = 1.0 / (1.0 + jnp.exp(-z))
        hidden = (z * sigma).astype(BF16)
        gz = (ga * sigma * (1.0 + z * (1.0 - sigma))).astype(BF16)
        a_out[b * span : (b + 1) * span, :] = hidden
        rim_first[b * PLANE : (b + 1) * PLANE, :] = hidden[0:PLANE]
        rim_last[b * PLANE : (b + 1) * PLANE, :] = hidden[span - PLANE : span]
        for dx in range(3):
            rows = slice(dx * PLANE, dx * PLANE + span)
            spread[0, b, rows, dx * LANES : (dx + 1) * LANES] = gz
            spread[1, b, rows, dx * LANES : (dx + 1) * LANES] = hidden
    sums = []
    for kind, cols in ((0, cols_a), (1, cols_g)):
        total = None
        for b in range(blocks):
            part = lax.dot_general(
                spread[kind, b], cols[b], (((0,), (0,)), ((), ())), preferred_element_type=F32
            )
            total = part if total is None else total + part
        sums.append(total)

    def matrix(j):
        if j < TAPS:
            dx, k = j // 9, j % 9
            block = sums[0][dx * LANES : (dx + 1) * LANES, k * LANES : (k + 1) * LANES]
            return block.T[0:width]
        t = 2 * TAPS - 1 - j
        dx, k = t // 9, t % 9
        return sums[1][dx * LANES : dx * LANES + width, k * LANES : (k + 1) * LANES]

    main, folded = fold_counts(width)
    lane = lax.broadcasted_iota(jnp.int32, (width, LANES), 1)
    room = LANES - width
    each = width // room
    for j in range(main):
        value = matrix(j)
        if j // each < folded:
            extra = matrix(main + j // each)
            chunk = j % each
            extra = pltpu.roll(extra, (width - room * chunk) % LANES, 1)
            value = jnp.where(lane < width, value, extra)
        terms[j * width : (j + 1) * width, :] = value.astype(BF16)
    for j in range(main + folded, 2 * TAPS):
        place = j - folded
        terms[place * width : (place + 1) * width, :] = matrix(j).astype(BF16)
    used = (2 * TAPS - folded) * width
    terms[used:, :] = jnp.zeros((terms.shape[0] - used, LANES), BF16)


def fold_counts(width):
    each = width // (LANES - width)
    folded = 2 * TAPS // (each + 1)
    return folded * each, folded


def sum_kernel(orders, sizes, terms, total, work, landing, whole, send_sem, recv_sem):
    place = {axis: lax.axis_index(axis) for axis in sizes}
    partners = {}
    for axis, bit in orders[0]:
        mine = (place[axis] // (1 << bit)) % 2
        partners[axis, bit] = (mine, place[axis] + (1 - 2 * mine) * (1 << bit))
    barrier = pltpu.get_barrier_semaphore()
    for (axis, _), (_, other) in partners.items():
        pl.semaphore_signal(
            barrier, inc=1, device_id={axis: other}, device_id_type=pl.DeviceIdType.MESH
        )
    pl.semaphore_wait(barrier, len(partners))

    steps = len(orders[0])
    rows = terms.shape[0] // len(orders)
    bases = [s * rows for s in range(len(orders))]
    at = [s * rows for s in range(len(orders))]
    length = rows

    def ds(start, size):
        return pl.ds(pl.multiple_of(start, 16), size)

    for step in range(steps):
        half = length // 2
        source = terms if step == 0 else work
        target = whole if step == steps - 1 else work
        copies = []
        for s, order in enumerate(orders):
            axis, bit = order[step]
            mine, other = partners[axis, bit]
            copy = pltpu.make_async_remote_copy(
                src_ref=source.at[ds(bases[s] + (1 - mine) * half, half)],
                dst_ref=landing.at[pl.ds(at[s], half)],
                send_sem=send_sem.at[s, step],
                recv_sem=recv_sem.at[s, step],
                device_id={axis: other},
                device_id_type=pl.DeviceIdType.MESH,
            )
            copy.start()
            copies.append(copy)
        for s, order in enumerate(orders):
            mine, _ = partners[order[step]]
            copies[s].wait()
            keep = bases[s] + mine * half
            value = source[ds(keep, half), :].astype(F32)
            value += landing[at[s] : at[s] + half, :].astype(F32)
            target[ds(keep, half), :] = value.astype(BF16)
            bases[s] = keep
            at[s] += half
        length = half
    for step in reversed(range(steps)):
        copies = []
        for s, order in enumerate(orders):
            axis, bit = order[step]
            _, other = partners[axis, bit]
            here = whole.at[ds(bases[s], length)]
            copy = pltpu.make_async_remote_copy(
                src_ref=here,
                dst_ref=here,
                send_sem=send_sem.at[s, steps + step],
                recv_sem=recv_sem.at[s, steps + step],
                device_id={axis: other},
                device_id_type=pl.DeviceIdType.MESH,
            )
            copy.start()
            copies.append(copy)
        for s, order in enumerate(orders):
            copies[s].wait()
            mine, _ = partners[order[step]]
            bases[s] = bases[s] - mine * length
        length *= 2
    total[...] = whole[...]


def last_kernel(
    blocks, width, scale, hidden, low_in, high_in, occ, two, near, total,
    out, grad_one, grad_two, local, rims, q, cols, weight,
):
    taps = 9 * LANES
    span = 8 * PLANE
    local[0:blocks] = hidden[...].astype(F32).reshape(blocks, 8, 8, 8, LANES)
    local[blocks] = jnp.zeros((8, 8, 8, LANES), F32)
    for side, arrived in ((0, low_in), (1, high_in)):
        rims[side, 0:blocks] = arrived[...].astype(F32).reshape(blocks, 8, 8, LANES)
        rims[side, blocks] = jnp.zeros((8, 8, LANES), F32)
    weight[...] = jnp.zeros_like(weight)
    for t in range(TAPS):
        weight[t * LANES : t * LANES + width, 0:width] = two[t]
    build_windows(blocks, local, rims.at[0], rims.at[1], near, q, cols)
    mask_row = (occ[...] > 0).astype(F32)
    for b in range(blocks):
        y = jnp.zeros((span, LANES), F32)
        for dx in range(3):
            y += jnp.dot(
                cols[b, dx * PLANE : dx * PLANE + span, :],
                weight[dx * taps : (dx + 1) * taps, :],
                preferred_element_type=F32,
            )
        here = slice(b * span, (b + 1) * span)
        out[:, here] = (y.T[0:width] * mask_row[:, here]).astype(BF16)

    main, folded = fold_counts(width)
    each = main // folded

    def rows(place):
        return total[place * width : (place + 1) * width, :].astype(F32) * scale

    def put(j, value):
        if j < TAPS:
            grad_one[j] = value
        else:
            grad_two[j - TAPS] = value

    for group in range(folded):
        spare = []
        for chunk in range(each):
            value = rows(group * each + chunk)
            put(group * each + chunk, value[:, 0:width])
            spare.append(value[:, width:LANES])
        put(main + group, jnp.concatenate(spare, axis=1))
    for j in range(main + folded, 2 * TAPS):
        put(j, rows(j - folded)[:, 0:width])


def bits_of(axis, size):
    return [(axis, bit) for bit in range(size.bit_length() - 1)]


def per_device(sizes, features_in, occupancy, cotangent, kernel_one, kernel_two, neighbours):
    width, span = features_in.shape
    blocks = neighbours.shape[0]
    devices = math.prod(sizes.values())
    scale = float(span * devices) ** (-0.5)
    vmem = pl.BlockSpec(memory_space=pltpu.VMEM)
    smem = pl.BlockSpec(memory_space=pltpu.SMEM)
    params = pltpu.CompilerParams(vmem_limit_bytes=48 * 1024 * 1024)
    occ = occupancy[None, :]
    count = sizes["dev"]
    forward = [(i, i + 1) for i in range(count - 1)]
    backward = [(target, source) for source, target in forward]

    def plane(values, x):
        return values.reshape(width, blocks, 8, PLANE)[:, :, x].reshape(width, -1)

    def rim(x):
        both = jnp.concatenate([plane(features_in, x), plane(cotangent, x)], axis=0)
        inside = occupancy.reshape(blocks, 8, PLANE)[:, x].reshape(1, -1) > 0
        return jnp.where(inside, both, jnp.zeros_like(both))

    low = lax.ppermute(rim(7), "dev", forward)
    high = lax.ppermute(rim(0), "dev", backward)

    orders = [
        bits_of("group", sizes["group"])[:1]
        + bits_of("dev", sizes["dev"])[:1]
        + bits_of("group", sizes["group"])[1:]
        + bits_of("dev", sizes["dev"])[1:],
        bits_of("group", sizes["group"]) + bits_of("dev", sizes["dev"]),
    ]
    steps = len(orders[0])
    streams = len(orders)
    _, folded = fold_counts(width)
    used = (2 * TAPS - folded) * width
    unit = 16 * devices * streams
    rows = -(-used // unit) * unit

    hidden, rim_first, rim_last, terms = pl.pallas_call(
        functools.partial(first_kernel, blocks, width),
        out_shape=(
            jax.ShapeDtypeStruct((span, LANES), BF16),
            jax.ShapeDtypeStruct((blocks * PLANE, LANES), BF16),
            jax.ShapeDtypeStruct((blocks * PLANE, LANES), BF16),
            jax.ShapeDtypeStruct((rows, LANES), BF16),
        ),
        in_specs=[vmem] * 7 + [smem],
        out_specs=[vmem] * 4,
        scratch_shapes=[
            pltpu.VMEM((2, blocks + 1, 8, 8, 8, LANES), F32),
            pltpu.VMEM((2, 2, blocks + 1, 8, 8, LANES), F32),
            pltpu.VMEM((3, blocks, 10, 10, 8, LANES), F32),
            pltpu.VMEM((blocks, 10 * PLANE, 9 * LANES), BF16),
            pltpu.VMEM((blocks, 10 * PLANE, 9 * LANES), BF16),
            pltpu.VMEM((TAPS * LANES, LANES), BF16),
            pltpu.VMEM((LANES, TAPS * LANES), BF16),
            pltpu.VMEM((2, blocks, 10 * PLANE, 3 * LANES), BF16),
        ],
        compiler_params=params,
        name="first_layer",
    )(features_in, cotangent, occ, low, high, kernel_one, kernel_two, neighbours)

    low = lax.ppermute(rim_last, "dev", forward)
    high = lax.ppermute(rim_first, "dev", backward)

    total = pl.pallas_call(
        functools.partial(sum_kernel, orders, sizes),
        out_shape=jax.ShapeDtypeStruct((rows, LANES), BF16),
        in_specs=[vmem],
        out_specs=vmem,
        scratch_shapes=[
            pltpu.VMEM((rows, LANES), BF16),
            pltpu.VMEM((rows, LANES), BF16),
            pltpu.VMEM((rows, LANES), BF16),
            pltpu.SemaphoreType.DMA((streams, 2 * steps)),
            pltpu.SemaphoreType.DMA((streams, 2 * steps)),
        ],
        compiler_params=pltpu.CompilerParams(
            collective_id=0, has_side_effects=True, vmem_limit_bytes=48 * 1024 * 1024
        ),
        name="sum_terms",
    )(terms)

    return pl.pallas_call(
        functools.partial(last_kernel, blocks, width, scale),
        out_shape=(
            jax.ShapeDtypeStruct((width, span), BF16),
            jax.ShapeDtypeStruct((TAPS, width, width), F32),
            jax.ShapeDtypeStruct((TAPS, width, width), F32),
        ),
        in_specs=[vmem] * 5 + [smem, vmem],
        out_specs=[vmem] * 3,
        scratch_shapes=[
            pltpu.VMEM((blocks + 1, 8, 8, 8, LANES), F32),
            pltpu.VMEM((2, blocks + 1, 8, 8, LANES), F32),
            pltpu.VMEM((3, blocks, 10, 10, 8, LANES), F32),
            pltpu.VMEM((blocks, 10 * PLANE, 9 * LANES), BF16),
            pltpu.VMEM((TAPS * LANES, LANES), BF16),
        ],
        compiler_params=params,
        name="second_layer",
    )(hidden, low, high, occ, kernel_two, neighbours, total)


def solution(mesh):
    sizes = dict(mesh.shape)
    return jax.shard_map(
        functools.partial(per_device, sizes),
        mesh=mesh,
        in_specs=(
            P(None, ("group", "dev")),
            P(("group", "dev")),
            P(None, ("group", "dev")),
            P(),
            P(),
            P(("group", "dev"), None),
        ),
        out_specs=(P(None, ("group", "dev")), P(), P()),
        check_vma=False,
    )
```

time: 269 us -> 73.4 us (0.27); the launches traced: 264 us -> 73.2 us
  waiting for transfers between devices: 151 us -> 4.69 us
  Pallas kernels: 0 us -> 51 us
  local copies, waits for them, and re-layouts: 40.2 us -> 4.74 us
  matrix products: 33 us -> 0 us
  between operations: 15.8 us -> 0.83 us
  other arithmetic: 9.91 us -> 0.07 us
    psum x1 -> x0, waiting for transfers between devices: 131 us -> none  [reduce_grad(): whole = lax.psum(flat, ('group', 'dev'))]
    pallas_call x0 -> x3, Pallas kernels: none -> 51 us  [the longest x1 37.9 us: per_device(): pl.pallas_call(functools.partial(sum_kernel, orders, sizes), out_shape=ja...]
    dot_general x45 -> x0, matrix products: 33 us -> none  [the longest x18 13.9 us: kernel_terms(): lax.dot_general(stacked, grad, (((1,), (1,)), ((), ())), preferred_elemen...]
    gather x5 -> x0, local copies, waits for them, and re-layouts: 17.5 us -> none  [the longest x3 14.4 us: padded_of(): return jnp.take(table, columns.reshape(-1), axis=1)]
    ppermute x4, waiting for transfers between devices: 19.6 us -> 4.69 us  [the longest x1 4.58 us: per_device(): high = lax.ppermute(rim(0), 'dev', backward)]
    slice x9 -> x2, local copies, waits for them, and re-layouts: 8.21 us -> 0.01 us  [plane(): return values.reshape(width, blocks, 8, PLANE)[:, :, x].reshape(width, -1)]
    unnamed x177 -> x14, local copies, waits for them, and re-layouts: 11.1 us -> 3.31 us
    concatenate x2 -> x0, other arithmetic: 4.97 us -> none  [padded_of(): jnp.concatenate([values, lower, upper, jnp.zeros((values.shape[0], 1), va...]
  transfers between devices with their start and end apart: 5 -> 4, of which waited for: 5 -> 2; matrix products, arithmetic and copies ran while one was open for 5% -> 0% of each run, Pallas kernels for 0% -> 52%
where the time goes in v1:
time: 73.4 us; the launch traced here: 73.2 us
  Pallas kernels  51 us (69%)
  starting transfers between devices  11.8 us (16%)
  local copies, waits for them, and re-layouts  4.74 us (6%)
  waiting for transfers between devices  4.69 us (6%)
  between operations  0.83 us (1%)
    pallas_call x1, Pallas kernels, per_device(): pl.pallas_call(functools.partial(sum_kernel, orders, sizes), out_shape=ja...  37.9 us
    pallas_call x1, Pallas kernels, per_device(): pl.pallas_call(functools.partial(first_kernel, blocks, width), out_shape=...  8.82 us
    ppermute x1, starting transfers between devices, per_device(): low = lax.ppermute(rim(7), 'dev', forward)  4.84 us
    ppermute x1, waiting for transfers between devices, per_device(): high = lax.ppermute(rim(0), 'dev', backward)  4.58 us
    ppermute x1, starting transfers between devices, per_device(): low = lax.ppermute(rim_last, 'dev', forward)  4.35 us
    pallas_call x1, Pallas kernels, per_device(): pl.pallas_call(functools.partial(last_kernel, blocks, width, scale), out_...  4.33 us
    unnamed x14, local copies, waits for them, and re-layouts  3.31 us
  transfers between devices with their start and end apart: 4, of which 2 were waited for; matrix products, arithmetic and copies ran while one was open for 0% of the time, Pallas kernels for 52%

profile of v1, /device:TPU:0, one launch (start us, length us, event | category | flops | bytes accessed | tf_op | source)
XLA Modules:
  0.0 73.2 jit_solution(18423660425745253116)
XLA Ops:
  0.6 0.0 copy-start.4
  0.6 0.0 copy-start.1
  0.7 0.0 copy-start.2
  0.7 0.0 copy-start.5
  0.7 0.0 copy-start
  0.7 0.8 %reshape.36 = s32[2,8,64]{2,1,0:T(8,128)S(1)} reshape(s32[1024]{0:T(1024)} %param.7) | data formatting | bytes 8192 | tf_op jit(solution)/shard_map/reshape | solution.py:308
  1.6 0.1 gt.23
  1.6 1.1 %copy.19 = bf16[96,1024]{0,1:T(8,128)(2,1)S(1)} copy(bf16[96,1024]{1,0:T(8,128)(2,1)} %feat.1) | data formatting | bytes 393216 | tf_op args[0]
  2.8 0.1 copy.21
  2.9 1.1 %copy.20 = bf16[96,1024]{0,1:T(8,128)(2,1)S(1)} copy(bf16[96,1024]{1,0:T(8,128)(2,1)} %cot.1) | data formatting | bytes 393216 | tf_op args[2]
  4.0 0.1 copy.22
  4.1 4.8 %collective-permute-start = (bf16[192,128]{1,0:T(8,128)(2,1)S(1)}, bf16[192,128]{1,0:T(8,128)(2,1)S(1)}, u32[]{:S(2)}, u32[]{:S(2)}) collective-permute-start(bf16[192,128]{1,0:T(8,128)(2,1)S(1)} %maximum_select_fusion), channel_id=1, source_target_pairs={{0,1},{1,2},{2,3},{3,4},{4,5},{5,6},{6,7},{8,9},{9,10},{10,11},{11... | collective-permute-start | bytes 147464 | tf_op jit(solution)/shard_map/ppermute | solution.py:311
  9.0 0.1 gt.25
  9.1 0.1 copy.23
  9.2 0.1 copy.24
  9.3 1.3 %collective-permute-start.1 = (bf16[192,128]{1,0:T(8,128)(2,1)S(1)}, bf16[192,128]{1,0:T(8,128)(2,1)S(1)}, u32[]{:S(2)}, u32[]{:S(2)}) collective-permute-start(bf16[192,128]{1,0:T(8,128)(2,1)S(1)} %maximum_select_fusion.1), channel_id=1, source_target_pairs={{1,0},{2,1},{3,2},{4,3},{5,4},{6,5},{7,6},{9,8},{10,9},{11,10},{12... | collective-permute-start | bytes 147464 | tf_op jit(solution)/shard_map/ppermute | solution.py:312
  10.6 0.1 collective-permute-done.low_in
  10.7 4.6 %collective-permute-done.1.high_in = bf16[192,128]{1,0:T(8,128)(2,1)S(1)} collective-permute-done((bf16[192,128]{1,0:T(8,128)(2,1)S(1)}, bf16[192,128]{1,0:T(8,128)(2,1)S(1)}, u32[]{:S(2)}, u32[]{:S(2)}) %collective-permute-start.1) | collective-permute-done | bytes 49184 | tf_op jit(solution)/shard_map/ppermute | solution.py:312
  15.3 0.0 copy-done.4
  15.3 0.0 copy-done.1
  15.3 0.0 copy-done.2
  15.3 0.0 copy-done.5
  15.3 0.0 copy-done
  15.3 0.0 copy-start.3
  15.3 1.1 %copy-done.3 = bf16[27,96,96]{2,1,0:T(8,128)(2,1)S(1)} copy-done((bf16[27,96,96]{2,1,0:T(8,128)(2,1)S(1)}, bf16[27,96,96]{2,1,0:T(8,128)(2,1)}, u32[]{:S(2)}) %copy-start.3) | copy-done | bytes 497688
  16.4 8.8 %first_layer.1 = (bf16[1024,128]{1,0:T(8,128)(2,1)S(1)}, bf16[128,128]{1,0:T(8,128)(2,1)S(1)}, bf16[128,128]{1,0:T(8,128)(2,1)S(1)}, bf16[4096,128]{1,0:T(8,128)(2,1)S(1)}) custom-call(bf16[96,1024]{1,0:T(8,128)(2,1)S(1)} %copy-done.1, bf16[96,1024]{1,0:T(8,128)(2,1)S(1)} %copy-done.2, s32[1,1024]{1,0:T(1,128)S(1)} %bitcast.7, ...), custom_call_target="tpu_custom_call" | custom-call | tf_op jit(solution)/shard_map/first_layer/pallas_call | solution.py:328
  25.2 4.4 %collective-permute-start.2 = (bf16[128,128]{1,0:T(8,128)(2,1)S(1)}, bf16[128,128]{1,0:T(8,128)(2,1)S(1)}, u32[]{:S(2)}, u32[]{:S(2)}) collective-permute-start(bf16[128,128]{1,0:T(8,128)(2,1)S(1)} %get-tuple-element.8), channel_id=1, source_target_pairs={{0,1},{1,2},{2,3},{3,4},{4,5},{5,6},{6,7},{8,9},{9,10},{10,11},{11... | collective-permute-start | bytes 98312 | tf_op jit(solution)/shard_map/ppermute | solution.py:352
  29.6 1.3 %collective-permute-start.3 = (bf16[128,128]{1,0:T(8,128)(2,1)S(1)}, bf16[128,128]{1,0:T(8,128)(2,1)S(1)}, u32[]{:S(2)}, u32[]{:S(2)}) collective-permute-start(bf16[128,128]{1,0:T(8,128)(2,1)S(1)} %get-tuple-element.9), channel_id=1, source_target_pairs={{1,0},{2,1},{3,2},{4,3},{5,4},{6,5},{7,6},{9,8},{10,9},{11,10},{12... | collective-permute-start | bytes 98312 | tf_op jit(solution)/shard_map/ppermute | solution.py:353
  30.9 37.9 %sum_terms.1.total = bf16[4096,128]{1,0:T(8,128)(2,1)S(1)} custom-call(bf16[4096,128]{1,0:T(8,128)(2,1)S(1)} %get-tuple-element.10.terms), custom_call_target="tpu_custom_call" | custom-call | tf_op jit(solution)/shard_map/sum_terms/pallas_call | solution.py:355
  68.8 0.0 collective-permute-done.2.low_in
  68.8 0.0 collective-permute-done.3.high_in
  68.8 4.3 %second_layer.1 = (bf16[96,1024]{1,0:T(8,128)(2,1)}, f32[27,96,96]{2,1,0:T(8,128)}, f32[27,96,96]{2,1,0:T(8,128)}) custom-call(bf16[1024,128]{1,0:T(8,128)(2,1)S(1)} %get-tuple-element.7.hidden, bf16[128,128]{1,0:T(8,128)(2,1)S(1)} %collective-permute-done.2.low_in, bf16[128,128]{1,0:T(8,128)(2,1)S(1)} %collective-permute-done.3.high_in, ...), custom_call_target="tpu_custom_call" | custom-call | tf_op jit(solution)/shard_map/second_layer/pallas_call | solution.py:373
  (5 shorter events, 0.1 us)
Async XLA Ops:
  0.6 14.7 %copy-start.4 = (s32[1024]{0:T(1024)S(1)}, s32[1024]{0:T(1024)}, u32[]{:S(2)}) copy-start(s32[1024]{0:T(1024)} %param.7) | copy-start | bytes 12292
  0.6 14.7 %copy-start.1 = (bf16[96,1024]{1,0:T(8,128)(2,1)S(1)}, bf16[96,1024]{1,0:T(8,128)(2,1)}, u32[]{:S(2)}) copy-start(bf16[96,1024]{1,0:T(8,128)(2,1)} %feat.1) | copy-start | bytes 589828
  0.7 14.6 %copy-start.2 = (bf16[96,1024]{1,0:T(8,128)(2,1)S(1)}, bf16[96,1024]{1,0:T(8,128)(2,1)}, u32[]{:S(2)}) copy-start(bf16[96,1024]{1,0:T(8,128)(2,1)} %cot.1) | copy-start | bytes 589828
  0.7 14.6 %copy-start.5 = (s32[2,27]{1,0:T(2,128)S(1)}, s32[2,27]{1,0:T(2,128)}, u32[]{:S(2)}) copy-start(s32[2,27]{1,0:T(2,128)} %near.3) | copy-start | bytes 652
  0.7 14.6 %copy-start = (bf16[27,96,96]{2,1,0:T(8,128)(2,1)S(1)}, bf16[27,96,96]{2,1,0:T(8,128)(2,1)}, u32[]{:S(2)}) copy-start(bf16[27,96,96]{2,1,0:T(8,128)(2,1)} %two.3) | copy-start | bytes 1492996
  4.1 6.6 %collective-permute-start = (bf16[192,128]{1,0:T(8,128)(2,1)S(1)}, bf16[192,128]{1,0:T(8,128)(2,1)S(1)}, u32[]{:S(2)}, u32[]{:S(2)}) collective-permute-start(bf16[192,128]{1,0:T(8,128)(2,1)S(1)} %maximum_select_fusion), channel_id=1, source_target_pairs={{0,1},{1,2},{2,3},{3,4},{4,5},{5,6},{6,7},{8,9},{9,10},{10,11},{11... | collective-permute-start | bytes 147464 | tf_op jit(solution)/shard_map/ppermute | solution.py:311
  9.3 6.0 %collective-permute-start.1 = (bf16[192,128]{1,0:T(8,128)(2,1)S(1)}, bf16[192,128]{1,0:T(8,128)(2,1)S(1)}, u32[]{:S(2)}, u32[]{:S(2)}) collective-permute-start(bf16[192,128]{1,0:T(8,128)(2,1)S(1)} %maximum_select_fusion.1), channel_id=1, source_target_pairs={{1,0},{2,1},{3,2},{4,3},{5,4},{6,5},{7,6},{9,8},{10,9},{11,10},{12... | collective-permute-start | bytes 147464 | tf_op jit(solution)/shard_map/ppermute | solution.py:312
  15.3 1.1 %copy-start.3 = (bf16[27,96,96]{2,1,0:T(8,128)(2,1)S(1)}, bf16[27,96,96]{2,1,0:T(8,128)(2,1)}, u32[]{:S(2)}) copy-start(bf16[27,96,96]{2,1,0:T(8,128)(2,1)} %one.1) | copy-start | bytes 1492996
  25.2 43.6 %collective-permute-start.2 = (bf16[128,128]{1,0:T(8,128)(2,1)S(1)}, bf16[128,128]{1,0:T(8,128)(2,1)S(1)}, u32[]{:S(2)}, u32[]{:S(2)}) collective-permute-start(bf16[128,128]{1,0:T(8,128)(2,1)S(1)} %get-tuple-element.8), channel_id=1, source_target_pairs={{0,1},{1,2},{2,3},{3,4},{4,5},{5,6},{6,7},{8,9},{9,10},{10,11},{11... | collective-permute-start | bytes 98312 | tf_op jit(solution)/shard_map/ppermute | solution.py:352
  29.6 39.2 %collective-permute-start.3 = (bf16[128,128]{1,0:T(8,128)(2,1)S(1)}, bf16[128,128]{1,0:T(8,128)(2,1)S(1)}, u32[]{:S(2)}, u32[]{:S(2)}) collective-permute-start(bf16[128,128]{1,0:T(8,128)(2,1)S(1)} %get-tuple-element.9), channel_id=1, source_target_pairs={{1,0},{2,1},{3,2},{4,3},{5,4},{6,5},{7,6},{9,8},{10,9},{11,10},{12... | collective-permute-start | bytes 98312 | tf_op jit(solution)/shard_map/ppermute | solution.py:353

commit v2 on v0

v2 whole, which is shorter than its diff:
```python
import functools
import math

import jax
import jax.numpy as jnp
from jax import lax
from jax.experimental import pallas as pl
from jax.experimental.pallas import tpu as pltpu
from jax.sharding import PartitionSpec as P

LANES = 128
TAPS = 27
PLANE = 64
F32 = jnp.float32
BF16 = jnp.bfloat16


def build_windows(blocks, local, lower, upper, near, q, cols):
    row = lax.broadcasted_iota(jnp.int32, (1, 8, LANES), 1)

    def shifted(main, before, after):
        down = jnp.where(row == 0, pltpu.roll(before, 1, 1), pltpu.roll(main, 1, 1))
        up = jnp.where(row == 7, pltpu.roll(after, 7, 1), pltpu.roll(main, 7, 1))
        return down, main, up

    for b in range(blocks):
        for tx in range(3):
            for ty in range(3):
                src_y = (slice(7, 8), slice(0, 8), slice(0, 1))[ty]
                dst_y = (slice(0, 1), slice(1, 9), slice(9, 10))[ty]
                dst_x = (slice(0, 1), slice(1, 9), slice(9, 10))[tx]
                rows_y = src_y.stop - src_y.start
                rows_x = dst_x.stop - dst_x.start
                parts = []
                for tz in range(3):
                    n = near[b, tx * 9 + ty * 3 + tz]
                    n = n - (blocks, 0, 2 * blocks)[tx]
                    index = jnp.where((n >= 0) & (n < blocks), n, blocks)
                    if tx == 1:
                        value = local[index, :, src_y]
                    else:
                        value = (lower, None, upper)[tx][index, src_y]
                    parts.append(value.reshape(rows_x * rows_y, 8, LANES))
                moved = shifted(parts[1], parts[0], parts[2])
                for dz in range(3):
                    q[dz, b, dst_x, dst_y] = moved[dz].reshape(rows_x, rows_y, 8, LANES)
        for dy in range(3):
            for dz in range(3):
                k = dy * 3 + dz
                window = q[dz, b, :, dy : dy + 8].reshape(10 * PLANE, LANES)
                cols[b, :, k * LANES : (k + 1) * LANES] = window.astype(BF16)


def tall(values, width):
    values = values.astype(F32)
    filler = jnp.zeros((LANES - width, values.shape[1]), F32)
    return jnp.concatenate([values, filler], axis=0).T


def fold_counts(width):
    each = width // (LANES - width)
    folded = TAPS // (each + 1)
    return folded * each, folded


def fold(terms, start, rows, width, matrix):
    main, folded = fold_counts(width)
    lane = lax.broadcasted_iota(jnp.int32, (width, LANES), 1)
    room = LANES - width
    each = width // room
    for j in range(main):
        chunk = j % each
        extra = pltpu.roll(matrix(main + j // each), (width - room * chunk) % LANES, 1)
        at = start + j * width
        terms[at : at + width, :] = jnp.where(lane < width, matrix(j), extra)
    for j in range(main + folded, TAPS):
        at = start + (j - folded) * width
        terms[at : at + width, :] = matrix(j)
    used = (TAPS - folded) * width
    terms[start + used : start + rows, :] = jnp.zeros((rows - used, LANES), F32)


class Stream:
    def __init__(self, number, start, rows, order, place, refs):
        self.number, self.base, self.length, self.order = number, start, rows, order
        self.at = start
        self.place = place
        self.terms, self.stage, self.landing, self.whole, self.send_sem, self.recv_sem = refs
        self.step = 0
        self.copies = []
        self.sent = []
        self.slot = 0

    def ds(self, start, size):
        return pl.ds(pl.multiple_of(start, 16), size)

    def send(self, src, dst, axis, other):
        copy = pltpu.make_async_remote_copy(
            src_ref=src,
            dst_ref=dst,
            send_sem=self.send_sem.at[self.number, self.slot],
            recv_sem=self.recv_sem.at[self.number, self.slot],
            device_id={axis: other},
            device_id_type=pl.DeviceIdType.MESH,
        )
        copy.start()
        self.slot += 1
        self.copies.append(copy)
        self.sent.append(copy)

    def start(self):
        count = len(self.order)
        self.copies = []
        if self.step < count:
            axis, low, radix = self.order[self.step]
            digit, others = peers(self.place, axis, low, radix)
            chunk = self.length // radix
            self.slots = []
            for theirs, other in others:
                here = slice(self.at, self.at + chunk)
                values = self.terms[self.ds(self.base + theirs * chunk, chunk), :]
                self.stage[here, :] = values.astype(BF16)
                rows = pl.ds(self.at, chunk)
                self.send(self.stage.at[rows], self.landing.at[rows], axis, other)
                self.slots.append(here)
                self.at += chunk
        else:
            axis, low, radix = self.order[2 * count - 1 - self.step]
            _, others = peers(self.place, axis, low, radix)
            here = self.whole.at[self.ds(self.base, self.length)]
            for _, other in others:
                self.send(here, here, axis, other)

    def finish(self):
        count = len(self.order)
        for copy in self.copies:
            copy.wait_recv()
        if self.step < count:
            axis, low, radix = self.order[self.step]
            digit, _ = peers(self.place, axis, low, radix)
            chunk = self.length // radix
            keep = self.base + digit * chunk
            value = self.terms[self.ds(keep, chunk), :]
            for here in self.slots:
                value = value + self.landing[here, :].astype(F32)
            if self.step == count - 1:
                self.whole[self.ds(keep, chunk), :] = value.astype(BF16)
            else:
                self.terms[self.ds(keep, chunk), :] = value
            self.base, self.length = keep, chunk
        else:
            axis, low, radix = self.order[2 * count - 1 - self.step]
            digit, _ = peers(self.place, axis, low, radix)
            self.base = self.base - digit * self.length
            self.length *= radix
        self.step += 1

    def done(self):
        return self.step == 2 * len(self.order)

    def advance(self):
        if not self.done():
            self.finish()
            if not self.done():
                self.start()

    def close(self):
        for copy in self.sent:
            copy.wait_send()


def peers(place, axis, low, radix):
    unit = 1 << low
    digit = (place[axis] // unit) % radix
    others = []
    for step in range(1, radix):
        theirs = (digit + step) % radix
        others.append((theirs, place[axis] + (theirs - digit) * unit))
    return digit, others


def step_kernel(
    blocks, width, sizes, orders, stream_rows,
    feat, cot, occ, one, two, near,
    out, total,
    local_a, local_g, low_a, high_a, low_g, high_g, q, cols_a, cols_g, weight_one, weight_two,
    spread_a, spread_g, send_first, send_last, land_low, land_high,
    hidden_first, hidden_last, hidden_low, hidden_high,
    terms, stage, landing, whole, send_sem, recv_sem, rim_send, rim_recv,
):
    taps = 9 * LANES
    span = 8 * PLANE
    rim_rows = blocks * PLANE
    place = {axis: lax.axis_index(axis) for axis in sizes}
    dev, count = place["dev"], sizes["dev"]
    has_low = dev > 0
    has_high = dev < count - 1
    low_dev = (dev + count - 1) % count
    high_dev = (dev + 1) % count

    for ref in (land_low, land_high, hidden_low, hidden_high):
        ref[...] = jnp.zeros_like(ref)

    barrier = pltpu.get_barrier_semaphore()

    def greet(axis, other):
        pl.semaphore_signal(
            barrier, inc=1, device_id={axis: other}, device_id_type=pl.DeviceIdType.MESH
        )

    greeted = 0
    for phase in orders[0]:
        for _, other in peers(place, *phase)[1]:
            greet(phase[0], other)
            greeted += 1

    @pl.when(has_low)
    def _():
        greet("dev", low_dev)

    @pl.when(has_high)
    def _():
        greet("dev", high_dev)

    def rim_copy(which, src, dst, other):
        return pltpu.make_async_remote_copy(
            src_ref=src,
            dst_ref=dst,
            send_sem=rim_send.at[which],
            recv_sem=rim_recv.at[which],
            device_id={"dev": other},
            device_id_type=pl.DeviceIdType.MESH,
        )

    rim_copies = [
        rim_copy(0, send_last, land_low, high_dev),
        rim_copy(1, send_first, land_high, low_dev),
        rim_copy(2, hidden_last, hidden_low, high_dev),
        rim_copy(3, hidden_first, hidden_high, low_dev),
    ]

    def rims_go(first):
        @pl.when(has_high)
        def _():
            rim_copies[first].start()

        @pl.when(has_low)
        def _():
            rim_copies[first + 1].start()

    def rims_here(first):
        @pl.when(has_low)
        def _():
            rim_copies[first].wait_recv()

        @pl.when(has_high)
        def _():
            rim_copies[first + 1].wait_recv()

    def rims_gone(first):
        @pl.when(has_high)
        def _():
            rim_copies[first].wait_send()

        @pl.when(has_low)
        def _():
            rim_copies[first + 1].wait_send()

    mask_row = (occ[...] > 0).astype(F32)
    for kind, source, local in ((0, feat, local_a), (1, cot, local_g)):
        value = tall(source[...].astype(F32) * mask_row, width)
        local[0:blocks] = value.reshape(blocks, 8, 8, 8, LANES)
        local[blocks] = jnp.zeros((8, 8, 8, LANES), F32)
        for b in range(blocks):
            at = kind * rim_rows + b * PLANE
            send_first[at : at + PLANE, :] = value[b * span : b * span + PLANE].astype(BF16)
            send_last[at : at + PLANE, :] = value[(b + 1) * span - PLANE : (b + 1) * span].astype(BF16)

    pl.semaphore_wait(barrier, greeted + has_low.astype(jnp.int32) + has_high.astype(jnp.int32))
    rims_go(0)

    mask = jnp.broadcast_to(mask_row, (LANES, blocks * span)).T
    weight_one[...] = jnp.zeros_like(weight_one)
    weight_two[...] = jnp.zeros_like(weight_two)
    for t in range(TAPS):
        weight_one[t * LANES : t * LANES + width, 0:width] = one[t]
        weight_two[0:width, t * LANES : t * LANES + width] = two[TAPS - 1 - t]
    spread_a[...] = jnp.zeros_like(spread_a)
    spread_g[...] = jnp.zeros_like(spread_g)

    def widen(arrived, start, rim):
        value = arrived[start : start + rim_rows, :].astype(F32)
        rim[0:blocks] = value.reshape(blocks, 8, 8, LANES)
        rim[blocks] = jnp.zeros((8, 8, LANES), F32)

    rims_here(0)
    for kind, low, high in ((0, low_a, high_a), (1, low_g, high_g)):
        widen(land_low, kind * rim_rows, low)
        widen(land_high, kind * rim_rows, high)

    refs = (terms, stage, landing, whole, send_sem, recv_sem)
    streams = [
        Stream(i, i * stream_rows, stream_rows, orders[i % 2], place, refs) for i in range(4)
    ]

    def conv(cols, weight, b):
        y = jnp.zeros((span, LANES), F32)
        for dx in range(3):
            y += jnp.dot(
                cols[b, dx * PLANE : dx * PLANE + span, :],
                weight[dx * taps : (dx + 1) * taps, :],
                preferred_element_type=F32,
            )
        return y

    def outer(spread, cols):
        sums = None
        for b in range(blocks):
            part = lax.dot_general(
                spread[b], cols[b], (((0,), (0,)), ((), ())), preferred_element_type=F32
            )
            sums = part if sums is None else sums + part
        return sums

    build_windows(blocks, local_a, low_a, high_a, near, q, cols_a)
    zs = []
    for b in range(blocks):
        here = slice(b * span, (b + 1) * span)
        z = conv(cols_a, weight_one, b) * mask[here]
        zs.append(z)
        hidden = (z * (1.0 / (1.0 + jnp.exp(-z)))).astype(BF16)
        hidden_first[b * PLANE : (b + 1) * PLANE, :] = hidden[0:PLANE]
        hidden_last[b * PLANE : (b + 1) * PLANE, :] = hidden[span - PLANE : span]
        local_a[b] = hidden.astype(F32).reshape(8, 8, 8, LANES)
        for dx in range(3):
            rows = slice(dx * PLANE, dx * PLANE + span)
            spread_a[b, rows, dx * LANES : (dx + 1) * LANES] = hidden
    rims_go(2)

    build_windows(blocks, local_g, low_g, high_g, near, q, cols_g)
    sums = outer(spread_a, cols_g)

    def second_matrix(j):
        dx, k = (TAPS - 1 - j) // 9, (TAPS - 1 - j) % 9
        return sums[dx * LANES : dx * LANES + width, k * LANES : (k + 1) * LANES]

    fold(terms, 0, 2 * stream_rows, width, second_matrix)
    for stream in streams[:2]:
        stream.start()

    for b in range(blocks):
        ga = jnp.zeros((span, LANES), F32)
        for dx in range(3):
            ga += lax.dot_general(
                cols_g[b, dx * PLANE : dx * PLANE + span, :],
                weight_two[:, dx * taps : (dx + 1) * taps],
                (((1,), (1,)), ((), ())),
                preferred_element_type=F32,
            )
        z = zs[b]
        ga = ga * mask[b * span : (b + 1) * span]
        sigma = 1.0 / (1.0 + jnp.exp(-z))
        gz = (ga * sigma * (1.0 + z * (1.0 - sigma))).astype(BF16)
        for dx in range(3):
            rows = slice(dx * PLANE, dx * PLANE + span)
            spread_g[b, rows, dx * LANES : (dx + 1) * LANES] = gz
    for stream in streams[:2]:
        stream.advance()
    crossed = outer(spread_g, cols_a)

    def first_matrix(j):
        dx, k = j // 9, j % 9
        return crossed[dx * LANES : (dx + 1) * LANES, k * LANES : (k + 1) * LANES].T[0:width]

    fold(terms, 2 * stream_rows, 2 * stream_rows, width, first_matrix)
    for stream in streams[2:]:
        stream.start()
    for stream in streams[:2]:
        stream.advance()

    rims_here(2)
    widen(hidden_low, 0, low_a)
    widen(hidden_high, 0, high_a)
    for t in range(TAPS):
        weight_one[t * LANES : t * LANES + width, 0:width] = two[t]
    build_windows(blocks, local_a, low_a, high_a, near, q, cols_a)
    for stream in streams:
        stream.advance()
    for b in range(blocks):
        here = slice(b * span, (b + 1) * span)
        y = conv(cols_a, weight_one, b)
        out[:, here] = (y.T[0:width] * mask_row[:, here]).astype(BF16)
        for stream in streams:
            stream.advance()
    while not all(stream.done() for stream in streams):
        for stream in streams:
            stream.advance()
    for stream in streams:
        stream.close()
    rims_gone(0)
    rims_gone(2)
    total[...] = whole[...]


def unfold_kernel(width, scale, total, grad_one, grad_two):
    main, folded = fold_counts(width)
    each = main // folded
    half = total.shape[0] // 2
    for start, grad in ((0, grad_two), (half, grad_one)):

        def rows(place):
            at = start + place * width
            return total[at : at + width, :].astype(F32) * scale

        for group in range(folded):
            spare = []
            for chunk in range(each):
                value = rows(group * each + chunk)
                grad[group * each + chunk] = value[:, 0:width]
                spare.append(value[:, width:LANES])
            grad[main + group] = jnp.concatenate(spare, axis=1)
        for j in range(main + folded, TAPS):
            grad[j] = rows(j - folded)[:, 0:width]


def phases_of(axis, size, first):
    bits = size.bit_length() - 1
    phases = []
    while first < bits:
        step = min(2, bits - first)
        phases.append((axis, first, 1 << step))
        first += step
    return phases


def per_device(sizes, features_in, occupancy, cotangent, kernel_one, kernel_two, neighbours):
    width, voxels = features_in.shape
    blocks = neighbours.shape[0]
    devices = math.prod(sizes.values())
    scale = float(voxels * devices) ** (-0.5)
    vmem = pl.BlockSpec(memory_space=pltpu.VMEM)
    smem = pl.BlockSpec(memory_space=pltpu.SMEM)
    limit = 56 * 1024 * 1024

    core = [("group", 0, 2)]
    beside = [("dev", 0, 2)]
    across = phases_of("group", sizes["group"], 1)
    along = phases_of("dev", sizes["dev"], 1)
    orders = [core + beside + across + along, core + across + beside + along]
    slots = 2 * sum(radix - 1 for _, _, radix in orders[0])
    _, folded = fold_counts(width)
    used = (TAPS - folded) * width
    unit = 16 * devices
    stream_rows = -(-used // (2 * unit)) * unit
    rows = 4 * stream_rows

    rim = pltpu.VMEM((blocks + 1, 8, 8, LANES), F32)
    cube = pltpu.VMEM((blocks + 1, 8, 8, 8, LANES), F32)
    cols = pltpu.VMEM((blocks, 10 * PLANE, 9 * LANES), BF16)
    spread = pltpu.VMEM((blocks, 10 * PLANE, 3 * LANES), BF16)
    both_rims = pltpu.VMEM((2 * blocks * PLANE, LANES), BF16)
    one_rim = pltpu.VMEM((blocks * PLANE, LANES), BF16)
    packed = pltpu.VMEM((rows, LANES), BF16)
    out, total = pl.pallas_call(
        functools.partial(step_kernel, blocks, width, sizes, orders, stream_rows),
        out_shape=(
            jax.ShapeDtypeStruct((width, voxels), BF16),
            jax.ShapeDtypeStruct((rows, LANES), BF16),
        ),
        in_specs=[vmem] * 5 + [smem],
        out_specs=[vmem] * 2,
        scratch_shapes=[cube, cube, rim, rim, rim, rim]
        + [pltpu.VMEM((3, blocks, 10, 10, 8, LANES), F32), cols, cols]
        + [pltpu.VMEM((TAPS * LANES, LANES), BF16), pltpu.VMEM((LANES, TAPS * LANES), BF16)]
        + [spread, spread]
        + [both_rims] * 4
        + [one_rim] * 4
        + [pltpu.VMEM((rows, LANES), F32), packed, packed, packed]
        + [pltpu.SemaphoreType.DMA((4, slots))] * 2
        + [pltpu.SemaphoreType.DMA((4,))] * 2,
        compiler_params=pltpu.CompilerParams(
            collective_id=0, has_side_effects=True, vmem_limit_bytes=limit
        ),
        name="train_step",
    )(features_in, cotangent, occupancy[None, :], kernel_one, kernel_two, neighbours)
    grad_one, grad_two = pl.pallas_call(
        functools.partial(unfold_kernel, width, scale),
        out_shape=(jax.ShapeDtypeStruct((TAPS, width, width), F32),) * 2,
        in_specs=[vmem],
        out_specs=[vmem] * 2,
        compiler_params=pltpu.CompilerParams(vmem_limit_bytes=limit),
        name="unfold",
    )(total)
    return out, grad_one, grad_two


def solution(mesh):
    sizes = dict(mesh.shape)
    return jax.shard_map(
        functools.partial(per_device, sizes),
        mesh=mesh,
        in_specs=(
            P(None, ("group", "dev")),
            P(("group", "dev")),
            P(None, ("group", "dev")),
            P(),
            P(),
            P(("group", "dev"), None),
        ),
        out_specs=(P(None, ("group", "dev")), P(), P()),
        check_vma=False,
    )
```

time: 269 us -> 54.2 us (0.20); the launches traced: 264 us -> 54 us
  waiting for transfers between devices: 151 us -> 0 us
  Pallas kernels: 0 us -> 51.7 us
  local copies, waits for them, and re-layouts: 40.2 us -> 1.62 us
  matrix products: 33 us -> 0 us
  between operations: 15.8 us -> 0.64 us
  starting transfers between devices: 14 us -> 0 us
  other arithmetic: 9.91 us -> 0 us
    psum x1 -> x0, waiting for transfers between devices: 131 us -> none  [reduce_grad(): whole = lax.psum(flat, ('group', 'dev'))]
    pallas_call x0 -> x2, Pallas kernels: none -> 51.7 us  [the longest x1 48.5 us: per_device(): pl.pallas_call(functools.partial(step_kernel, blocks, width, sizes, order...]
    dot_general x45 -> x0, matrix products: 33 us -> none  [the longest x18 13.9 us: kernel_terms(): lax.dot_general(stacked, grad, (((1,), (1,)), ((), ())), preferred_elemen...]
    ppermute x4 -> x0, waiting for transfers between devices: 19.6 us -> none  [the longest x2 15.6 us: with_halo(): lax.ppermute(lax.slice_in_dim(block, block.shape[dim] - width, None, axis...]
    gather x5 -> x0, local copies, waits for them, and re-layouts: 17.5 us -> none  [the longest x3 14.4 us: padded_of(): return jnp.take(table, columns.reshape(-1), axis=1)]
    ppermute x4 -> x0, starting transfers between devices: 14 us -> none  [the longest x2 11.4 us: with_halo(): lax.ppermute(lax.slice_in_dim(block, block.shape[dim] - width, None, axis...]
    unnamed x177 -> x1, local copies, waits for them, and re-layouts: 11.1 us -> 1.62 us
    slice x9 -> x0, local copies, waits for them, and re-layouts: 8.21 us -> none  [the longest x6 6.39 us: cube_window(): cube[:, :, first:first + 8, second:second + 8, third:third + 8]]
  transfers between devices with their start and end apart: 5 -> 0, of which waited for: 5 -> 0; matrix products, arithmetic and copies ran while one was open for 5% -> 0% of each run, Pallas kernels for 0% -> 0%
where the time goes in v2:
time: 54.2 us; the launch traced here: 54 us
  Pallas kernels  51.7 us (95%)
  local copies, waits for them, and re-layouts  1.62 us (3%)
  between operations  0.64 us (1%)
    pallas_call x1, Pallas kernels, per_device(): pl.pallas_call(functools.partial(step_kernel, blocks, width, sizes, order...  48.5 us
    pallas_call x1, Pallas kernels, per_device(): pl.pallas_call(functools.partial(unfold_kernel, width, scale), out_shape=...  3.19 us
    unnamed x1, local copies, waits for them, and re-layouts  1.62 us

profile of v2, /device:TPU:0, one launch (start us, length us, event | category | flops | bytes accessed | tf_op | source)
XLA Modules:
  0.0 54.0 jit_solution(16209188559147917602)
XLA Ops:
  0.6 48.5 %train_step.1 = (bf16[96,1024]{1,0:T(8,128)(2,1)}, bf16[4096,128]{1,0:T(8,128)(2,1)}) custom-call(bf16[96,1024]{1,0:T(8,128)(2,1)} %feat.1, bf16[96,1024]{1,0:T(8,128)(2,1)} %cot.1, s32[1,1024]{1,0:T(1,128)} %bitcast.1, bf16[27,96,96]{2,1,0:T(8,128)(2,1)} %one.1, bf16[27,96,96]{2,1,0:T(8,128)(2,1)} %two.1, s32[2,27]{1,0:T(2,128)} %near.1), custom_call_target="tpu_custom_call" | custom-call | tf_op jit(solution)/shard_map/train_step/pallas_call | solution.py:464
  49.1 3.2 %unfold.1 = (f32[27,96,96]{2,1,0:T(8,128)}, f32[27,96,96]{2,1,0:T(8,128)}) custom-call(bf16[4096,128]{1,0:T(8,128)(2,1)} %get-tuple-element.8.total), custom_call_target="tpu_custom_call" | custom-call | tf_op jit(solution)/shard_map/unfold/pallas_call | solution.py:486
  52.3 1.6 %copy.10 = bf16[96,1024]{1,0:T(8,128)(2,1)} copy(bf16[96,1024]{1,0:T(8,128)(2,1)} %get-tuple-element.14) | data formatting | bytes 393216

commit v3 on v2

--- a/solution.py
+++ b/solution.py
@@ -15,7 +15,7 @@
 BF16 = jnp.bfloat16
 
 
-def build_windows(blocks, local, lower, upper, near, q, cols):
+def build_windows(blocks, local, lower, upper, near, q, cols, inner):
     row = lax.broadcasted_iota(jnp.int32, (1, 8, LANES), 1)
 
     def shifted(main, before, after):
@@ -24,7 +24,7 @@
         return down, main, up
 
     for b in range(blocks):
-        for tx in range(3):
+        for tx in (1,) if inner else (0, 2):
             for ty in range(3):
                 src_y = (slice(7, 8), slice(0, 8), slice(0, 1))[ty]
                 dst_y = (slice(0, 1), slice(1, 9), slice(9, 10))[ty]
@@ -47,8 +47,10 @@
         for dy in range(3):
             for dz in range(3):
                 k = dy * 3 + dz
-                window = q[dz, b, :, dy : dy + 8].reshape(10 * PLANE, LANES)
-                cols[b, :, k * LANES : (k + 1) * LANES] = window.astype(BF16)
+                for x, end in ((1, 9),) if inner else ((0, 1), (9, 10)):
+                    window = q[dz, b, x:end, dy : dy + 8].reshape((end - x) * PLANE, LANES)
+                    lanes = slice(k * LANES, (k + 1) * LANES)
+                    cols[b, x * PLANE : end * PLANE, lanes] = window.astype(BF16)
 
 
 def tall(values, width):
@@ -181,8 +183,9 @@
 
 def step_kernel(
     blocks, width, sizes, orders, stream_rows,
-    feat, cot, occ, one, two, near,
+    feat_far, cot_far, one_far, two_far, occ, near,
     out, total,
+    feat, cot, one, two, in_sem, part_z, part_g,
     local_a, local_g, low_a, high_a, low_g, high_g, q, cols_a, cols_g, weight_one, weight_two,
     spread_a, spread_g, send_first, send_last, land_low, land_high,
     hidden_first, hidden_last, hidden_low, hidden_high,
@@ -198,6 +201,14 @@
     low_dev = (dev + count - 1) % count
     high_dev = (dev + 1) % count
 
+    loads = [
+        pltpu.make_async_copy(src, dst, in_sem.at[i])
+        for i, (src, dst) in enumerate(
+            ((feat_far, feat), (cot_far, cot), (one_far, one), (two_far, two))
+        )
+    ]
+    for load in loads:
+        load.start()
     for ref in (land_low, land_high, hidden_low, hidden_high):
         ref[...] = jnp.zeros_like(ref)
 
@@ -267,6 +278,8 @@
             rim_copies[first + 1].wait_send()
 
     mask_row = (occ[...] > 0).astype(F32)
+    loads[0].wait()
+    loads[1].wait()
     for kind, source, local in ((0, feat, local_a), (1, cot, local_g)):
         value = tall(source[...].astype(F32) * mask_row, width)
         local[0:blocks] = value.reshape(blocks, 8, 8, 8, LANES)
@@ -282,6 +295,8 @@
     mask = jnp.broadcast_to(mask_row, (LANES, blocks * span)).T
     weight_one[...] = jnp.zeros_like(weight_one)
     weight_two[...] = jnp.zeros_like(weight_two)
+    loads[2].wait()
+    loads[3].wait()
     for t in range(TAPS):
         weight_one[t * LANES : t * LANES + width, 0:width] = one[t]
         weight_two[0:width, t * LANES : t * LANES + width] = two[TAPS - 1 - t]
@@ -293,6 +308,36 @@
         rim[0:blocks] = value.reshape(blocks, 8, 8, LANES)
         rim[blocks] = jnp.zeros((8, 8, LANES), F32)
 
+    def conv(cols, weight, b, steps):
+        y = None
+        for dx in steps:
+            term = jnp.dot(
+                cols[b, dx * PLANE : dx * PLANE + span, :],
+                weight[dx * taps : (dx + 1) * taps, :],
+                preferred_element_type=F32,
+            )
+            y = term if y is None else y + term
+        return y
+
+    def conv_back(b, steps):
+        y = None
+        for dx in steps:
+            term = lax.dot_general(
+                cols_g[b, dx * PLANE : dx * PLANE + span, :],
+                weight_two[:, dx * taps : (dx + 1) * taps],
+                (((1,), (1,)), ((), ())),
+                preferred_element_type=F32,
+            )
+            y = term if y is None else y + term
+        return y
+
+    build_windows(blocks, local_a, low_a, high_a, near, q, cols_a, True)
+    for b in range(blocks):
+        part_z[b] = conv(cols_a, weight_one, b, (1,))
+    build_windows(blocks, local_g, low_g, high_g, near, q, cols_g, True)
+    for b in range(blocks):
+        part_g[b] = conv_back(b, (1,))
+
     rims_here(0)
     for kind, low, high in ((0, low_a, high_a), (1, low_g, high_g)):
         widen(land_low, kind * rim_rows, low)
@@ -302,16 +347,6 @@
     streams = [
         Stream(i, i * stream_rows, stream_rows, orders[i % 2], place, refs) for i in range(4)
     ]
-
-    def conv(cols, weight, b):
-        y = jnp.zeros((span, LANES), F32)
-        for dx in range(3):
-            y += jnp.dot(
-                cols[b, dx * PLANE : dx * PLANE + span, :],
-                weight[dx * taps : (dx + 1) * taps, :],
-                preferred_element_type=F32,
-            )
-        return y
 
     def outer(spread, cols):
         sums = None
@@ -322,11 +357,11 @@
             sums = part if sums is None else sums + part
         return sums
 
-    build_windows(blocks, local_a, low_a, high_a, near, q, cols_a)
+    build_windows(blocks, local_a, low_a, high_a, near, q, cols_a, False)
     zs = []
     for b in range(blocks):
         here = slice(b * span, (b + 1) * span)
-        z = conv(cols_a, weight_one, b) * mask[here]
+        z = (part_z[b] + conv(cols_a, weight_one, b, (0, 2))) * mask[here]
         zs.append(z)
         hidden = (z * (1.0 / (1.0 + jnp.exp(-z)))).astype(BF16)
         hidden_first[b * PLANE : (b + 1) * PLANE, :] = hidden[0:PLANE]
@@ -337,7 +372,7 @@
             spread_a[b, rows, dx * LANES : (dx + 1) * LANES] = hidden
     rims_go(2)
 
-    build_windows(blocks, local_g, low_g, high_g, near, q, cols_g)
+    build_windows(blocks, local_g, low_g, high_g, near, q, cols_g, False)
     sums = outer(spread_a, cols_g)
 
     def second_matrix(j):
@@ -349,14 +384,7 @@
         stream.start()
 
     for b in range(blocks):
-        ga = jnp.zeros((span, LANES), F32)
-        for dx in range(3):
-            ga += lax.dot_general(
-                cols_g[b, dx * PLANE : dx * PLANE + span, :],
-                weight_two[:, dx * taps : (dx + 1) * taps],
-                (((1,), (1,)), ((), ())),
-                preferred_element_type=F32,
-            )
+        ga = part_g[b] + conv_back(b, (0, 2))
         z = zs[b]
         ga = ga * mask[b * span : (b + 1) * span]
         sigma = 1.0 / (1.0 + jnp.exp(-z))
@@ -383,12 +411,13 @@
     widen(hidden_high, 0, high_a)
     for t in range(TAPS):
         weight_one[t * LANES : t * LANES + width, 0:width] = two[t]
-    build_windows(blocks, local_a, low_a, high_a, near, q, cols_a)
+    build_windows(blocks, local_a, low_a, high_a, near, q, cols_a, True)
+    build_windows(blocks, local_a, low_a, high_a, near, q, cols_a, False)
     for stream in streams:
         stream.advance()
     for b in range(blocks):
         here = slice(b * span, (b + 1) * span)
-        y = conv(cols_a, weight_one, b)
+        y = conv(cols_a, weight_one, b, (0, 1, 2))
         out[:, here] = (y.T[0:width] * mask_row[:, here]).astype(BF16)
         for stream in streams:
             stream.advance()
@@ -402,7 +431,8 @@
     total[...] = whole[...]
 
 
-def unfold_kernel(width, scale, total, grad_one, grad_two):
+def unfold_kernel(width, scale, total, features, out, grad_one, grad_two):
+    out[...] = features[...]
     main, folded = fold_counts(width)
     each = main // folded
     half = total.shape[0] // 2
@@ -461,15 +491,19 @@
     both_rims = pltpu.VMEM((2 * blocks * PLANE, LANES), BF16)
     one_rim = pltpu.VMEM((blocks * PLANE, LANES), BF16)
     packed = pltpu.VMEM((rows, LANES), BF16)
-    out, total = pl.pallas_call(
+    features, total = pl.pallas_call(
         functools.partial(step_kernel, blocks, width, sizes, orders, stream_rows),
         out_shape=(
             jax.ShapeDtypeStruct((width, voxels), BF16),
             jax.ShapeDtypeStruct((rows, LANES), BF16),
         ),
-        in_specs=[vmem] * 5 + [smem],
+        in_specs=[pl.BlockSpec(memory_space=pl.ANY)] * 4 + [vmem, smem],
         out_specs=[vmem] * 2,
-        scratch_shapes=[cube, cube, rim, rim, rim, rim]
+        scratch_shapes=[pltpu.VMEM((width, voxels), BF16)] * 2
+        + [pltpu.VMEM((TAPS, width, width), BF16)] * 2
+        + [pltpu.SemaphoreType.DMA((4,))]
+        + [pltpu.VMEM((blocks, 8 * PLANE, LANES), F32)] * 2
+        + [cube, cube, rim, rim, rim, rim]
         + [pltpu.VMEM((3, blocks, 10, 10, 8, LANES), F32), cols, cols]
         + [pltpu.VMEM((TAPS * LANES, LANES), BF16), pltpu.VMEM((LANES, TAPS * LANES), BF16)]
         + [spread, spread]
@@ -482,16 +516,19 @@
             collective_id=0, has_side_effects=True, vmem_limit_bytes=limit
         ),
         name="train_step",
-    )(features_in, cotangent, occupancy[None, :], kernel_one, kernel_two, neighbours)
-    grad_one, grad_two = pl.pallas_call(
+    )(features_in, cotangent, kernel_one, kernel_two, occupancy[None, :], neighbours)
+    return pl.pallas_call(
         functools.partial(unfold_kernel, width, scale),
-        out_shape=(jax.ShapeDtypeStruct((TAPS, width, width), F32),) * 2,
-        in_specs=[vmem],
-        out_specs=[vmem] * 2,
-        compiler_params=pltpu.CompilerParams(vmem_limit_bytes=limit),
+        out_shape=(
+            jax.ShapeDtypeStruct((width, voxels), BF16),
+            jax.ShapeDtypeStruct((TAPS, width, width), F32),
+            jax.ShapeDtypeStruct((TAPS, width, width), F32),
+        ),
+        in_specs=[vmem] * 2,
+        out_specs=[vmem] * 3,
+        compiler_params=pltpu.CompilerParams(vmem_limit_bytes=16 * 1024 * 1024),
         name="unfold",
-    )(total)
-    return out, grad_one, grad_two
+    )(total, features)
 
 
 def solution(mesh):

time: 54.2 us -> 51.5 us (0.950)
  Pallas kernels: 51.7 us -> 48.5 us
    pallas_call x1, Pallas kernels: 48.5 us -> 46.5 us  [per_device(): pl.pallas_call(functools.partial(step_kernel, blocks, width, sizes, order...]
    pallas_call x1, Pallas kernels: 3.19 us -> 2.03 us  [per_device(): pl.pallas_call(functools.partial(unfold_kernel, width, scale), out_shape=...]
    unnamed x1 -> x4, local copies, waits for them, and re-layouts: 1.62 us -> 2.14 us
where the time goes in v3:
time: 51.5 us; the launch traced here: 51.3 us
  Pallas kernels  48.5 us (94%)
  local copies, waits for them, and re-layouts  2.14 us (4%)
  between operations  0.65 us (1%)
    pallas_call x1, Pallas kernels, per_device(): pl.pallas_call(functools.partial(step_kernel, blocks, width, sizes, order...  46.5 us
    unnamed x4, local copies, waits for them, and re-layouts  2.14 us
    pallas_call x1, Pallas kernels, per_device(): pl.pallas_call(functools.partial(unfold_kernel, width, scale), out_shape=...  2.03 us

profile of v3, /device:TPU:0, one launch (start us, length us, event | category | flops | bytes accessed | tf_op | source)
XLA Modules:
  0.0 51.3 jit_solution(10977273074738988032)
XLA Ops:
  0.6 46.5 %train_step.1 = (bf16[96,1024]{1,0:T(8,128)(2,1)}, bf16[4096,128]{1,0:T(8,128)(2,1)}) custom-call(bf16[96,1024]{1,0:T(8,128)(2,1)} %feat_far.1, bf16[96,1024]{1,0:T(8,128)(2,1)} %cot_far.1, bf16[27,96,96]{2,1,0:T(8,128)(2,1)} %one_far.1, bf16[27,96,96]{2,1,0:T(8,128)(2,1)} %two_far.1, s32[1,1024]{1,0:T(1,128)} %bitcast.1, s32[2,27]{1,0:T(2,128)} %near.1), custom_call_target="tpu_custom_call" | custom-call | tf_op jit(solution)/shard_map/train_step/pallas_call | solution.py:494
  47.1 0.0 copy-start
  47.1 1.2 %copy-done = bf16[4096,128]{1,0:T(8,128)(2,1)S(1)} copy-done((bf16[4096,128]{1,0:T(8,128)(2,1)S(1)}, bf16[4096,128]{1,0:T(8,128)(2,1)}, u32[]{:S(2)}) %copy-start) | copy-done | bytes 1048600
  48.3 0.0 copy-start.1
  48.3 0.9 %copy-done.1 = bf16[96,1024]{1,0:T(8,128)(2,1)S(1)} copy-done((bf16[96,1024]{1,0:T(8,128)(2,1)S(1)}, bf16[96,1024]{1,0:T(8,128)(2,1)}, u32[]{:S(2)}) %copy-start.1) | copy-done | bytes 196632
  49.3 2.0 %unfold.1 = (bf16[96,1024]{1,0:T(8,128)(2,1)}, f32[27,96,96]{2,1,0:T(8,128)}, f32[27,96,96]{2,1,0:T(8,128)}) custom-call(bf16[4096,128]{1,0:T(8,128)(2,1)S(1)} %copy-done, bf16[96,1024]{1,0:T(8,128)(2,1)S(1)} %copy-done.1), custom_call_target="tpu_custom_call" | custom-call | tf_op jit(solution)/shard_map/unfold/pallas_call | solution.py:520
Async XLA Ops:
  47.1 1.2 %copy-start = (bf16[4096,128]{1,0:T(8,128)(2,1)S(1)}, bf16[4096,128]{1,0:T(8,128)(2,1)}, u32[]{:S(2)}) copy-start(bf16[4096,128]{1,0:T(8,128)(2,1)} %get-tuple-element.5.total) | copy-start | bytes 3145732
  48.3 0.9 %copy-start.1 = (bf16[96,1024]{1,0:T(8,128)(2,1)S(1)}, bf16[96,1024]{1,0:T(8,128)(2,1)}, u32[]{:S(2)}) copy-start(bf16[96,1024]{1,0:T(8,128)(2,1)} %get-tuple-element.6.features) | copy-start | bytes 589828

commit v4 on v3

--- a/solution.py
+++ b/solution.py
@@ -184,8 +184,8 @@
 def step_kernel(
     blocks, width, sizes, orders, stream_rows,
     feat_far, cot_far, one_far, two_far, occ, near,
-    out, total,
-    feat, cot, one, two, in_sem, part_z, part_g,
+    out_far, total_far,
+    out, out_sem, feat, cot, one, two, in_sem, part_z, part_g,
     local_a, local_g, low_a, high_a, low_g, high_g, q, cols_a, cols_g, weight_one, weight_two,
     spread_a, spread_g, send_first, send_last, land_low, land_high,
     hidden_first, hidden_last, hidden_low, hidden_high,
@@ -421,22 +421,49 @@
         out[:, here] = (y.T[0:width] * mask_row[:, here]).astype(BF16)
         for stream in streams:
             stream.advance()
+    stores = [pltpu.make_async_copy(out, out_far, out_sem.at[0])]
+    stores[0].start()
+
+    def store_half(which):
+        rows = pl.ds(which * 2 * stream_rows, 2 * stream_rows)
+        store = pltpu.make_async_copy(whole.at[rows], total_far.at[rows], out_sem.at[1 + which])
+        store.start()
+        stores.append(store)
+
+    while not all(stream.done() for stream in streams[:2]):
+        for stream in streams:
+            stream.advance()
+    store_half(0)
     while not all(stream.done() for stream in streams):
         for stream in streams:
             stream.advance()
+    store_half(1)
     for stream in streams:
         stream.close()
     rims_gone(0)
     rims_gone(2)
-    total[...] = whole[...]
-
-
-def unfold_kernel(width, scale, total, features, out, grad_one, grad_two):
-    out[...] = features[...]
+    for store in stores:
+        store.wait()
+
+
+def unfold_kernel(
+    width, scale, total_far, features_far, out_far, one_far, two_far, total, grad_one, grad_two, sem
+):
     main, folded = fold_counts(width)
     each = main // folded
     half = total.shape[0] // 2
-    for start, grad in ((0, grad_two), (half, grad_one)):
+    loads = [
+        pltpu.make_async_copy(
+            total_far.at[pl.ds(i * half, half)], total.at[pl.ds(i * half, half)], sem.at[i]
+        )
+        for i in range(2)
+    ]
+    stores = [pltpu.make_async_copy(features_far, out_far, sem.at[2])]
+    for copy in loads + stores:
+        copy.start()
+    for i, grad, far in ((0, grad_two, two_far), (1, grad_one, one_far)):
+        start = i * half
+        loads[i].wait()
 
         def rows(place):
             at = start + place * width
@@ -451,6 +478,11 @@
             grad[main + group] = jnp.concatenate(spare, axis=1)
         for j in range(main + folded, TAPS):
             grad[j] = rows(j - folded)[:, 0:width]
+        store = pltpu.make_async_copy(grad, far, sem.at[3 + i])
+        store.start()
+        stores.append(store)
+    for store in stores:
+        store.wait()
 
 
 def phases_of(axis, size, first):
@@ -498,8 +530,9 @@
             jax.ShapeDtypeStruct((rows, LANES), BF16),
         ),
         in_specs=[pl.BlockSpec(memory_space=pl.ANY)] * 4 + [vmem, smem],
-        out_specs=[vmem] * 2,
-        scratch_shapes=[pltpu.VMEM((width, voxels), BF16)] * 2
+        out_specs=[pl.BlockSpec(memory_space=pl.ANY)] * 2,
+        scratch_shapes=[pltpu.VMEM((width, voxels), BF16), pltpu.SemaphoreType.DMA((3,))]
+        + [pltpu.VMEM((width, voxels), BF16)] * 2
         + [pltpu.VMEM((TAPS, width, width), BF16)] * 2
         + [pltpu.SemaphoreType.DMA((4,))]
         + [pltpu.VMEM((blocks, 8 * PLANE, LANES), F32)] * 2
@@ -524,9 +557,12 @@
             jax.ShapeDtypeStruct((TAPS, width, width), F32),
             jax.ShapeDtypeStruct((TAPS, width, width), F32),
         ),
-        in_specs=[vmem] * 2,
-        out_specs=[vmem] * 3,
-        compiler_params=pltpu.CompilerParams(vmem_limit_bytes=16 * 1024 * 1024),
+        in_specs=[pl.BlockSpec(memory_space=pl.ANY)] * 2,
+        out_specs=[pl.BlockSpec(memory_space=pl.ANY)] * 3,
+        scratch_shapes=[pltpu.VMEM((rows, LANES), BF16)]
+        + [pltpu.VMEM((TAPS, width, width), F32)] * 2
+        + [pltpu.SemaphoreType.DMA((5,))],
+        compiler_params=pltpu.CompilerParams(vmem_limit_bytes=limit),
         name="unfold",
     )(total, features)
 

time: 51.5 us -> 54.1 us (1.050); the launches traced: 51.3 us -> 53.2 us
  Pallas kernels: 48.5 us -> 52.5 us
  local copies, waits for them, and re-layouts: 2.14 us -> 0 us
    pallas_call x1, Pallas kernels: 2.03 us -> 7.11 us  [per_device(): pl.pallas_call(functools.partial(unfold_kernel, width, scale), out_shape=...]
    unnamed x4 -> x0, local copies, waits for them, and re-layouts: 2.14 us -> none
    pallas_call x1, Pallas kernels: 46.5 us -> 45.4 us  [per_device(): pl.pallas_call(functools.partial(step_kernel, blocks, width, sizes, order...]
where the time goes in v4:
time: 54.1 us; the launch traced here: 53.2 us
  Pallas kernels  52.5 us (97%)
  between operations  0.64 us (1%)
    pallas_call x1, Pallas kernels, per_device(): pl.pallas_call(functools.partial(step_kernel, blocks, width, sizes, order...  45.4 us
    pallas_call x1, Pallas kernels, per_device(): pl.pallas_call(functools.partial(unfold_kernel, width, scale), out_shape=...  7.11 us

profile of v4, /device:TPU:0, one launch (start us, length us, event | category | flops | bytes accessed | tf_op | source)
XLA Modules:
  0.0 53.2 jit_solution(14276410284199213694)
XLA Ops:
  0.6 45.4 %train_step.1 = (bf16[96,1024]{1,0:T(8,128)(2,1)}, bf16[4096,128]{1,0:T(8,128)(2,1)}) custom-call(bf16[96,1024]{1,0:T(8,128)(2,1)} %feat_far.1, bf16[96,1024]{1,0:T(8,128)(2,1)} %cot_far.1, bf16[27,96,96]{2,1,0:T(8,128)(2,1)} %one_far.1, bf16[27,96,96]{2,1,0:T(8,128)(2,1)} %two_far.1, s32[1,1024]{1,0:T(1,128)} %bitcast.1, s32[2,27]{1,0:T(2,128)} %near.1), custom_call_target="tpu_custom_call" | custom-call | tf_op jit(solution)/shard_map/train_step/pallas_call | solution.py:526
  46.1 7.1 %unfold.1 = (bf16[96,1024]{1,0:T(8,128)(2,1)}, f32[27,96,96]{2,1,0:T(8,128)}, f32[27,96,96]{2,1,0:T(8,128)}) custom-call(bf16[4096,128]{1,0:T(8,128)(2,1)} %get-tuple-element.5.total_far, bf16[96,1024]{1,0:T(8,128)(2,1)} %get-tuple-element.6.features_far), custom_call_target="tpu_custom_call" | custom-call | tf_op jit(solution)/shard_map/unfold/pallas_call | solution.py:553

commit v5 on v4

--- a/solution.py
+++ b/solution.py
@@ -447,7 +447,7 @@
 
 
 def unfold_kernel(
-    width, scale, total_far, features_far, out_far, one_far, two_far, total, grad_one, grad_two, sem
+    width, scale, total_far, features, out, one_far, two_far, total, grad_one, grad_two, sem
 ):
     main, folded = fold_counts(width)
     each = main // folded
@@ -458,9 +458,10 @@
         )
         for i in range(2)
     ]
-    stores = [pltpu.make_async_copy(features_far, out_far, sem.at[2])]
-    for copy in loads + stores:
+    stores = []
+    for copy in loads:
         copy.start()
+    out[...] = features[...]
     for i, grad, far in ((0, grad_two, two_far), (1, grad_one, one_far)):
         start = i * half
         loads[i].wait()
@@ -478,7 +479,7 @@
             grad[main + group] = jnp.concatenate(spare, axis=1)
         for j in range(main + folded, TAPS):
             grad[j] = rows(j - folded)[:, 0:width]
-        store = pltpu.make_async_copy(grad, far, sem.at[3 + i])
+        store = pltpu.make_async_copy(grad, far, sem.at[2 + i])
         store.start()
         stores.append(store)
     for store in stores:
@@ -557,11 +558,11 @@
             jax.ShapeDtypeStruct((TAPS, width, width), F32),
             jax.ShapeDtypeStruct((TAPS, width, width), F32),
         ),
-        in_specs=[pl.BlockSpec(memory_space=pl.ANY)] * 2,
-        out_specs=[pl.BlockSpec(memory_space=pl.ANY)] * 3,
+        in_specs=[pl.BlockSpec(memory_space=pl.ANY), vmem],
+        out_specs=[vmem] + [pl.BlockSpec(memory_space=pl.ANY)] * 2,
         scratch_shapes=[pltpu.VMEM((rows, LANES), BF16)]
         + [pltpu.VMEM((TAPS, width, width), F32)] * 2
-        + [pltpu.SemaphoreType.DMA((5,))],
+        + [pltpu.SemaphoreType.DMA((4,))],
         compiler_params=pltpu.CompilerParams(vmem_limit_bytes=limit),
         name="unfold",
     )(total, features)

time: 54.1 us -> 51.5 us (0.952)
  Pallas kernels: 52.5 us -> 49.9 us
    pallas_call x1, Pallas kernels: 7.11 us -> 4.48 us  [per_device(): pl.pallas_call(functools.partial(unfold_kernel, width, scale), out_shape=...]
where the time goes in v5:
time: 51.5 us; the launch traced here: 50.5 us
  Pallas kernels  49.9 us (97%)
  between operations  0.64 us (1%)
    pallas_call x1, Pallas kernels, per_device(): pl.pallas_call(functools.partial(step_kernel, blocks, width, sizes, order...  45.4 us
    pallas_call x1, Pallas kernels, per_device(): pl.pallas_call(functools.partial(unfold_kernel, width, scale), out_shape=...  4.48 us

profile of v5, /device:TPU:0, one launch (start us, length us, event | category | flops | bytes accessed | tf_op | source)
XLA Modules:
  0.0 50.5 jit_solution(1853379619524736010)
XLA Ops:
  0.6 45.4 %train_step.1 = (bf16[96,1024]{1,0:T(8,128)(2,1)}, bf16[4096,128]{1,0:T(8,128)(2,1)}) custom-call(bf16[96,1024]{1,0:T(8,128)(2,1)} %feat_far.1, bf16[96,1024]{1,0:T(8,128)(2,1)} %cot_far.1, bf16[27,96,96]{2,1,0:T(8,128)(2,1)} %one_far.1, bf16[27,96,96]{2,1,0:T(8,128)(2,1)} %two_far.1, s32[1,1024]{1,0:T(1,128)} %bitcast.1, s32[2,27]{1,0:T(2,128)} %near.1), custom_call_target="tpu_custom_call" | custom-call | tf_op jit(solution)/shard_map/train_step/pallas_call | solution.py:527
  46.1 4.5 %unfold.1 = (bf16[96,1024]{1,0:T(8,128)(2,1)}, f32[27,96,96]{2,1,0:T(8,128)}, f32[27,96,96]{2,1,0:T(8,128)}) custom-call(bf16[4096,128]{1,0:T(8,128)(2,1)} %get-tuple-element.5.total_far, bf16[96,1024]{1,0:T(8,128)(2,1)} %get-tuple-element.6.features), custom_call_target="tpu_custom_call" | custom-call | tf_op jit(solution)/shard_map/unfold/pallas_call | solution.py:554
